TPU v7x, 32 devices: a whole 2x2x4 slice. The times are simulated.
32 devices in a mesh: dp: 8 (over y, x, core), seq: 4 (over z).
Axes of the slice: x: 2, y: 2, z: 4, core: 2. Of those that a mesh axis runs over, the one named last changes fastest.
Arguments:
- tokens: bfloat16 [32, 1024, 768], P('dp', 'seq'), may hold values from -8 to 8
- doc_lengths: int32 [32, 4], P('dp'), may hold values from 1 to 768, 1024 in all within a row
- query_weight: bfloat16 [768, 768], P(('dp', 'seq')), may hold values from -0.21875 to 0.21875
- key_weight: bfloat16 [768, 768], P(('dp', 'seq')), may hold values from -0.21875 to 0.21875
- value_weight: bfloat16 [768, 768], P(('dp', 'seq')), may hold values from -0.21875 to 0.21875
- out_weight: bfloat16 [768, 768], P(('dp', 'seq')), may hold values from -1.75 to 1.75
- pool_weight: bfloat16 [10, 768], P(None, ('dp', 'seq')), may hold values from -2.5 to 2.5
- first_gain: bfloat16 [768], P(('dp', 'seq')), may hold values from 0.5 to 1.5
- first_shift: bfloat16 [768], P(('dp', 'seq')), may hold values from -1.25 to 1.25
- inner_weight: bfloat16 [768, 3072], P(('dp', 'seq')), may hold values from -0.21875 to 0.21875
- inner_bias: bfloat16 [3072], P(('dp', 'seq')), may hold values from -1.75 to 1.75
- outer_weight: bfloat16 [3072, 768], P(('dp', 'seq')), may hold values from -0.21875 to 0.21875
- outer_bias: bfloat16 [768], P(('dp', 'seq')), may hold values from -1.25 to 1.25
- second_gain: bfloat16 [768], P(('dp', 'seq')), may hold values from 0.5 to 1.5
- second_shift: bfloat16 [768], P(('dp', 'seq')), may hold values from -1.25 to 1.25
- cotangent: bfloat16 [32, 1024, 768], P('dp', 'seq'), may hold values from -6 to 6
Outputs:
- block_output: bfloat16 [32, 1024, 768], P('dp', 'seq')
- input_grad: bfloat16 [32, 1024, 768], P('dp', 'seq')
- query_grad: float32 [768, 768], P(('dp', 'seq'))
- key_grad: float32 [768, 768], P(('dp', 'seq'))
- value_grad: float32 [768, 768], P(('dp', 'seq'))
- out_grad: float32 [768, 768], P(('dp', 'seq'))
- pool_grad: float32 [10, 768], P(None, ('dp', 'seq'))
- first_gain_grad: float32 [768], P(('dp', 'seq'))
- first_shift_grad: float32 [768], P(('dp', 'seq'))
- inner_grad: float32 [768, 3072], P(('dp', 'seq'))
- inner_bias_grad: float32 [3072], P(('dp', 'seq'))
- outer_grad: float32 [3072, 768], P(('dp', 'seq'))
- outer_bias_grad: float32 [768], P(('dp', 'seq'))
- second_gain_grad: float32 [768], P(('dp', 'seq'))
- second_shift_grad: float32 [768], P(('dp', 'seq'))
Inputs may be any that keep to these rules, and one draw needn't show every extreme that they name: `doc_lengths`: each row's 4 lengths sum to 1024; the largest of each row is exactly 768.
All inputs are finite; a program needn't handle non-finite values.
Results may differ from a plain program's by a relative error of at most 0.015.
The roundings to bfloat16 on the way count: a program that leaves them out, or rounds other values in their place, can miss the bound.
Values may be sent and summed in bfloat16 or wider, within the bound.
No kernel may reach another device: no remote copies, remote signals or barrier semaphores. Data moves between devices by JAX's collectives and lax.ppermute only.
A program may use at most 256 MiB of HBM per device.

v0:
```python
import jax
import jax.numpy as jnp
from jax import lax
from jax.sharding import PartitionSpec as P

HEADS = 12
HEAD_DIM = 64
WIN = 128
PWIN = 512
MICRO = 2


EPS = 1e-05


def extended(cells, sides, width):
    for axis, dim in sides:
        count = lax.axis_size(axis)
        ends = count - 1
        head = lax.slice_in_dim(cells, 0, width, axis=dim)
        tail = lax.slice_in_dim(cells, cells.shape[dim] - width, cells.shape[dim], axis=dim)
        cells = jnp.concatenate(
            [
                lax.ppermute(tail, axis, [(i, (i + 1) % count) for i in range(ends)]),
                cells,
                lax.ppermute(head, axis, [((i + 1) % count, i) for i in range(ends)]),
            ],
            axis=dim,
        )
    return cells


def layer_norm(value, gain, shift):
    row_mean = jnp.mean(value, axis=-1, keepdims=True)
    centered = value - row_mean
    scaled = centered * lax.rsqrt(jnp.mean(centered * centered, axis=-1, keepdims=True) + EPS)
    return scaled * gain + shift


def gelu_exact(value):
    return jax.nn.gelu(value, approximate=False)


def document_of(positions, lengths, seq_len):
    ends = jnp.cumsum(lengths, axis=1)
    counted = jnp.sum((positions[None, :, None] >= ends[:, None, :]).astype(jnp.int32), axis=2)
    inside = (positions >= 0) & (positions < seq_len)
    return jnp.where(inside[None, :], counted, -1)


def dot_left(left, right):
    return lax.dot_general(
        left, right, (((0,), (0,)), ((), ())), preferred_element_type=jnp.float32
    )


def dot_right(left, right):
    return lax.dot_general(
        left, right, (((1,), (1,)), ((), ())), preferred_element_type=jnp.float32
    )


def add_earlier(earlier, later):
    if earlier is None:
        return later
    return tuple((first + second for first, second in zip(earlier, later)))


def run_micro(weights, tokens, lengths, cotangent, seq_place, seq_count):
    (
        w_query,
        w_key,
        w_value,
        w_out,
        w_pool,
        gain_one,
        shift_one,
        w_inner,
        bias_inner,
        w_outer,
        bias_outer,
        gain_two,
        shift_two,
    ) = weights
    seq_num, group_len, model_width = tokens.shape
    row_count = seq_num * group_len
    half_win = WIN // 2
    slot_half = PWIN // 8
    slot_count = group_len // 4
    slot_ext = slot_count + 2 * slot_half
    seq_len = group_len * seq_count
    scale = HEAD_DIM ** (-0.5)
    offset = seq_place * group_len
    flat_in = tokens.reshape(row_count, model_width)
    queries = jnp.dot(flat_in, w_query, preferred_element_type=jnp.float32).astype(jnp.bfloat16)
    key_rows = jnp.dot(flat_in, w_key, preferred_element_type=jnp.float32).astype(jnp.bfloat16)
    value_rows = jnp.dot(flat_in, w_value, preferred_element_type=jnp.float32).astype(jnp.bfloat16)
    pair = jnp.stack((key_rows, value_rows)).reshape(2, seq_num, group_len, model_width)
    pair_ext = extended(pair, (("seq", 2),), half_win)
    tok_pos = offset - half_win + jnp.arange(group_len + WIN, dtype=jnp.int32)
    tok_doc = document_of(tok_pos, lengths, seq_len)
    query_doc = tok_doc[:, half_win : half_win + group_len]
    front = (
        pair_ext[:, :, half_win : half_win + group_len]
        .astype(jnp.float32)
        .reshape(2, seq_num, slot_count, 4, model_width)
    )
    last_tap = (
        pair_ext[:, :, half_win + 4 : half_win + 4 + group_len]
        .astype(jnp.float32)
        .reshape(2, seq_num, slot_count, 4, model_width)[:, :, :, :1]
    )
    taps = jnp.concatenate((front, last_tap), axis=3)
    doc_front = query_doc.reshape(seq_num, slot_count, 4)
    doc_last = tok_doc[:, half_win + 4 : half_win + 4 + group_len].reshape(seq_num, slot_count, 4)[
        :, :, :1
    ]
    tap_doc = jnp.concatenate((doc_front, doc_last), axis=2)
    same_doc = (tap_doc == tap_doc[:, :, 2:3]).astype(jnp.float32)
    pool_taps = w_pool.astype(jnp.float32).reshape(2, 5, model_width)
    masked_taps = taps * same_doc[None, :, :, :, None]
    pooled = jnp.sum(masked_taps * pool_taps[:, None, None], axis=3).astype(jnp.bfloat16)
    pooled_ext = extended(pooled, (("seq", 2),), slot_half)
    slot_ids = seq_place * slot_count - slot_half + jnp.arange(slot_ext, dtype=jnp.int32)
    centers = 4 * slot_ids + 2
    slot_doc = document_of(centers, lengths, seq_len)
    query_pos = offset + jnp.arange(group_len, dtype=jnp.int32)
    near_band = jnp.abs(tok_pos[None, :] - query_pos[:, None]) <= half_win
    near_mask = near_band[None] & (query_doc[:, :, None] == tok_doc[:, None, :])
    far_band = jnp.abs(centers[None, :] - query_pos[:, None]) <= PWIN // 2
    far_mask = far_band[None] & (query_doc[:, :, None] == slot_doc[:, None, :])
    query_heads = queries.reshape(seq_num, group_len, HEADS, HEAD_DIM)
    key_ext = pair_ext[0].reshape(seq_num, group_len + WIN, HEADS, HEAD_DIM)
    value_ext = pair_ext[1].reshape(seq_num, group_len + WIN, HEADS, HEAD_DIM)
    pool_key = pooled_ext[0].reshape(seq_num, slot_ext, HEADS, HEAD_DIM)
    pool_value = pooled_ext[1].reshape(seq_num, slot_ext, HEADS, HEAD_DIM)
    near_scores = (
        jnp.einsum("sqhe,skhe->shqk", query_heads, key_ext, preferred_element_type=jnp.float32)
        * scale
    )
    far_scores = (
        jnp.einsum("sqhe,skhe->shqk", query_heads, pool_key, preferred_element_type=jnp.float32)
        * scale
    )
    near_scores = jnp.where(near_mask[:, None], near_scores, -1e30)
    far_scores = jnp.where(far_mask[:, None], far_scores, -1e30)
    top = jnp.maximum(
        jnp.max(near_scores, axis=3, keepdims=True), jnp.max(far_scores, axis=3, keepdims=True)
    )
    near_exp = jnp.exp(near_scores - top)
    far_exp = jnp.exp(far_scores - top)
    denom = jnp.sum(near_exp, axis=3, keepdims=True) + jnp.sum(far_exp, axis=3, keepdims=True)
    near_prob = near_exp / denom
    far_prob = far_exp / denom
    near_low = near_prob.astype(jnp.bfloat16)
    far_low = far_prob.astype(jnp.bfloat16)
    mixed = jnp.einsum("shqk,skhe->sqhe", near_low, value_ext, preferred_element_type=jnp.float32)
    mixed = mixed + jnp.einsum(
        "shqk,skhe->sqhe", far_low, pool_value, preferred_element_type=jnp.float32
    )
    mixed_low = mixed.reshape(row_count, model_width).astype(jnp.bfloat16)
    attended = jnp.dot(mixed_low, w_out, preferred_element_type=jnp.float32)
    first_sum = flat_in.astype(jnp.float32) + attended
    normed_one, pull_one = jax.vjp(
        layer_norm, first_sum, gain_one.astype(jnp.float32), shift_one.astype(jnp.float32)
    )
    normed_low = normed_one.astype(jnp.bfloat16)
    inner_pre = jnp.dot(
        normed_low, w_inner, preferred_element_type=jnp.float32
    ) + bias_inner.astype(jnp.float32)
    hidden, pull_gelu = jax.vjp(gelu_exact, inner_pre)
    hidden_low = hidden.astype(jnp.bfloat16)
    outer_pre = jnp.dot(
        hidden_low, w_outer, preferred_element_type=jnp.float32
    ) + bias_outer.astype(jnp.float32)
    output, pull_two = jax.vjp(
        layer_norm,
        normed_one + outer_pre,
        gain_two.astype(jnp.float32),
        shift_two.astype(jnp.float32),
    )
    cot_flat = cotangent.reshape(row_count, model_width).astype(jnp.float32)
    d_second, d_gain_two, d_shift_two = pull_two(cot_flat)
    d_outer = d_second.astype(jnp.bfloat16)
    d_outer_bias = jnp.sum(d_outer.astype(jnp.float32), axis=0)
    d_outer_weight = dot_left(hidden_low, d_outer)
    d_hidden = dot_right(d_outer, w_outer)
    (d_inner_pre,) = pull_gelu(d_hidden)
    d_inner = d_inner_pre.astype(jnp.bfloat16)
    d_inner_bias = jnp.sum(d_inner.astype(jnp.float32), axis=0)
    d_inner_weight = dot_left(normed_low, d_inner)
    d_normed = dot_right(d_inner, w_inner) + d_second
    d_first, d_gain_one, d_shift_one = pull_one(d_normed)
    ffn_piece = (
        d_gain_one,
        d_shift_one,
        d_inner_weight,
        d_inner_bias,
        d_outer_weight,
        d_outer_bias,
        d_gain_two,
        d_shift_two,
    )
    d_attended = d_first.astype(jnp.bfloat16)
    d_out_weight = dot_left(mixed_low, d_attended)
    d_mixed = (
        dot_right(d_attended, w_out)
        .astype(jnp.bfloat16)
        .reshape(seq_num, group_len, HEADS, HEAD_DIM)
    )
    d_near_prob = jnp.einsum(
        "sqhe,skhe->shqk", d_mixed, value_ext, preferred_element_type=jnp.float32
    )
    d_far_prob = jnp.einsum(
        "sqhe,skhe->shqk", d_mixed, pool_value, preferred_element_type=jnp.float32
    )
    d_value_ext = jnp.einsum(
        "shqk,sqhe->skhe", near_low, d_mixed, preferred_element_type=jnp.float32
    )
    d_pool_value = jnp.einsum(
        "shqk,sqhe->skhe", far_low, d_mixed, preferred_element_type=jnp.float32
    )
    row_dot = jnp.sum(near_prob * d_near_prob, axis=3, keepdims=True) + jnp.sum(
        far_prob * d_far_prob, axis=3, keepdims=True
    )
    d_near = (near_prob * (d_near_prob - row_dot)).astype(jnp.bfloat16)
    d_far = (far_prob * (d_far_prob - row_dot)).astype(jnp.bfloat16)
    d_query = jnp.einsum("shqk,skhe->sqhe", d_near, key_ext, preferred_element_type=jnp.float32)
    d_query = (
        d_query + jnp.einsum("shqk,skhe->sqhe", d_far, pool_key, preferred_element_type=jnp.float32)
    ) * scale
    d_key_ext = (
        jnp.einsum("shqk,sqhe->skhe", d_near, query_heads, preferred_element_type=jnp.float32)
        * scale
    )
    d_pool_key = (
        jnp.einsum("shqk,sqhe->skhe", d_far, query_heads, preferred_element_type=jnp.float32)
        * scale
    )
    d_pooled_ext = jnp.stack(
        (
            d_pool_key.reshape(seq_num, slot_ext, model_width),
            d_pool_value.reshape(seq_num, slot_ext, model_width),
        )
    )
    slot_edges = jnp.concatenate(
        (d_pooled_ext[:, :, :slot_half], d_pooled_ext[:, :, slot_ext - slot_half :]), axis=2
    )
    slot_came = extended(slot_edges.astype(jnp.bfloat16), (("seq", 2),), slot_half).astype(
        slot_edges.dtype
    )
    d_pooled = d_pooled_ext[:, :, slot_half : slot_half + slot_count]
    d_pooled = d_pooled + slot_came[:, :, :slot_half]
    d_pooled = d_pooled + slot_came[:, :, 3 * slot_half :]
    d_pool_weight = jnp.sum(d_pooled[:, :, :, None, :] * masked_taps, axis=(1, 2)).reshape(
        10, model_width
    )
    d_taps = d_pooled[:, :, :, None, :] * same_doc[None, :, :, :, None] * pool_taps[:, None, None]
    spread_front = d_taps[:, :, :, :4].reshape(2, seq_num, group_len, model_width)
    spread_last = jnp.concatenate(
        (d_taps[:, :, :, 4:], jnp.zeros((2, seq_num, slot_count, 3, model_width), jnp.float32)),
        axis=3,
    )
    spread_last = spread_last.reshape(2, seq_num, group_len, model_width)
    d_pair_ext = jnp.stack(
        (
            d_key_ext.reshape(seq_num, group_len + WIN, model_width),
            d_value_ext.reshape(seq_num, group_len + WIN, model_width),
        )
    )
    d_pair_ext = d_pair_ext + jnp.pad(spread_front, ((0, 0), (0, 0), (half_win, half_win), (0, 0)))
    d_pair_ext = d_pair_ext + jnp.pad(
        spread_last, ((0, 0), (0, 0), (half_win + 4, half_win - 4), (0, 0))
    )
    tok_edges = jnp.concatenate(
        (d_pair_ext[:, :, :half_win], d_pair_ext[:, :, group_len + half_win :]), axis=2
    )
    tok_came = extended(tok_edges.astype(jnp.bfloat16), (("seq", 2),), half_win).astype(
        tok_edges.dtype
    )
    d_pair = d_pair_ext[:, :, half_win : half_win + group_len]
    d_pair = d_pair + jnp.pad(
        tok_came[:, :, :half_win], ((0, 0), (0, 0), (0, group_len - half_win), (0, 0))
    )
    d_pair = d_pair + jnp.pad(
        tok_came[:, :, 3 * half_win :], ((0, 0), (0, 0), (group_len - half_win, 0), (0, 0))
    )
    d_key_low = d_pair[0].reshape(row_count, model_width).astype(jnp.bfloat16)
    d_value_low = d_pair[1].reshape(row_count, model_width).astype(jnp.bfloat16)
    d_query_low = d_query.reshape(row_count, model_width).astype(jnp.bfloat16)
    d_query_weight = dot_left(flat_in, d_query_low)
    d_key_weight = dot_left(flat_in, d_key_low)
    d_value_weight = dot_left(flat_in, d_value_low)
    d_input = (
        dot_right(d_query_low, w_query)
        + dot_right(d_key_low, w_key)
        + dot_right(d_value_low, w_value)
        + d_first
    )
    grad_piece = (
        d_query_weight,
        d_key_weight,
        d_value_weight,
        d_out_weight,
        d_pool_weight,
    ) + tuple(ffn_piece)
    out_piece = output.astype(jnp.bfloat16).reshape(seq_num, group_len, model_width)
    d_piece = d_input.astype(jnp.bfloat16).reshape(seq_num, group_len, model_width)
    return (out_piece, d_piece, grad_piece)


def local(
    tokens,
    doc_lengths,
    query_weight,
    key_weight,
    value_weight,
    out_weight,
    pool_weight,
    first_gain,
    first_shift,
    inner_weight,
    inner_bias,
    outer_weight,
    outer_bias,
    second_gain,
    second_shift,
    cotangent,
):
    shards = (
        query_weight,
        key_weight,
        value_weight,
        out_weight,
        pool_weight,
        first_gain,
        first_shift,
        inner_weight,
        inner_bias,
        outer_weight,
        outer_bias,
        second_gain,
        second_shift,
    )
    seq_count = lax.axis_size("seq")
    seq_place = lax.axis_index("seq")
    micro_seqs = tokens.shape[0] // MICRO
    grad_total = None
    out_pieces = []
    d_pieces = []
    for micro_step in range(MICRO):
        gathered = (
            lax.all_gather(shards[0], ("dp", "seq"), axis=0, tiled=True),
            lax.all_gather(shards[1], ("dp", "seq"), axis=0, tiled=True),
            lax.all_gather(shards[2], ("dp", "seq"), axis=0, tiled=True),
            lax.all_gather(shards[3], ("dp", "seq"), axis=0, tiled=True),
            lax.all_gather(shards[4], ("dp", "seq"), axis=1, tiled=True),
            lax.all_gather(shards[5], ("dp", "seq"), axis=0, tiled=True),
            lax.all_gather(shards[6], ("dp", "seq"), axis=0, tiled=True),
            lax.all_gather(shards[7], ("dp", "seq"), axis=0, tiled=True),
            lax.all_gather(shards[8], ("dp", "seq"), axis=0, tiled=True),
            lax.all_gather(shards[9], ("dp", "seq"), axis=0, tiled=True),
            lax.all_gather(shards[10], ("dp", "seq"), axis=0, tiled=True),
            lax.all_gather(shards[11], ("dp", "seq"), axis=0, tiled=True),
            lax.all_gather(shards[12], ("dp", "seq"), axis=0, tiled=True),
        )
        first_row = micro_step * micro_seqs
        last_row = first_row + micro_seqs
        out_piece, d_piece, grad_piece = run_micro(
            gathered,
            tokens[first_row:last_row],
            doc_lengths[first_row:last_row],
            cotangent[first_row:last_row],
            seq_place,
            seq_count,
        )
        out_pieces.append(out_piece)
        d_pieces.append(d_piece)
        grad_total = add_earlier(grad_total, grad_piece)
    summed = (
        lax.psum_scatter(grad_total[0], ("dp", "seq"), scatter_dimension=0, tiled=True),
        lax.psum_scatter(grad_total[1], ("dp", "seq"), scatter_dimension=0, tiled=True),
        lax.psum_scatter(grad_total[2], ("dp", "seq"), scatter_dimension=0, tiled=True),
        lax.psum_scatter(grad_total[3], ("dp", "seq"), scatter_dimension=0, tiled=True),
        lax.psum_scatter(grad_total[4], ("dp", "seq"), scatter_dimension=1, tiled=True),
        lax.psum_scatter(grad_total[5], ("dp", "seq"), scatter_dimension=0, tiled=True),
        lax.psum_scatter(grad_total[6], ("dp", "seq"), scatter_dimension=0, tiled=True),
        lax.psum_scatter(grad_total[7], ("dp", "seq"), scatter_dimension=0, tiled=True),
        lax.psum_scatter(grad_total[8], ("dp", "seq"), scatter_dimension=0, tiled=True),
        lax.psum_scatter(grad_total[9], ("dp", "seq"), scatter_dimension=0, tiled=True),
        lax.psum_scatter(grad_total[10], ("dp", "seq"), scatter_dimension=0, tiled=True),
        lax.psum_scatter(grad_total[11], ("dp", "seq"), scatter_dimension=0, tiled=True),
        lax.psum_scatter(grad_total[12], ("dp", "seq"), scatter_dimension=0, tiled=True),
    )
    block_output = jnp.concatenate(out_pieces, axis=0)
    input_grad = jnp.concatenate(d_pieces, axis=0)
    return (
        block_output,
        input_grad,
        summed[0],
        summed[1],
        summed[2],
        summed[3],
        summed[4],
        summed[5],
        summed[6],
        summed[7],
        summed[8],
        summed[9],
        summed[10],
        summed[11],
        summed[12],
    )


def solution(mesh):
    in_specs = (
        P("dp", "seq", None),
        P("dp", None),
        P(("dp", "seq"), None),
        P(("dp", "seq"), None),
        P(("dp", "seq"), None),
        P(("dp", "seq"), None),
        P(None, ("dp", "seq")),
        P(("dp", "seq")),
        P(("dp", "seq")),
        P(("dp", "seq"), None),
        P(("dp", "seq")),
        P(("dp", "seq"), None),
        P(("dp", "seq")),
        P(("dp", "seq")),
        P(("dp", "seq")),
        P("dp", "seq", None),
    )
    out_specs = (
        P("dp", "seq", None),
        P("dp", "seq", None),
        P(("dp", "seq"), None),
        P(("dp", "seq"), None),
        P(("dp", "seq"), None),
        P(("dp", "seq"), None),
        P(None, ("dp", "seq")),
        P(("dp", "seq")),
        P(("dp", "seq")),
        P(("dp", "seq"), None),
        P(("dp", "seq")),
        P(("dp", "seq"), None),
        P(("dp", "seq")),
        P(("dp", "seq")),
        P(("dp", "seq")),
    )
    return jax.shard_map(local, mesh=mesh, in_specs=in_specs, out_specs=out_specs, check_vma=False)
```

profile of v0, /device:TPU:16, one launch (start us, length us, event | category | flops | bytes accessed | tf_op | source)
XLA Modules:
  0.0 1219.3 jit_solution(16061168241219856310)
XLA Ops:
  18.1 65.7 %all-gather = bf16[32,24,10]{1,2,0:T(8,128)(2,1)S(1)} all-gather(bf16[1,24,10]{1,2,0:T(8,128)(2,1)S(1)} %bitcast.320), channel_id=1, replica_groups=mesh['dp'=8,'seq'=4] {'dp','seq'}, dimensions={0}, use_global_device_ids=true | all-gather | bytes 15840 | tf_op jit(solution)/shard_map/all_gather | solution.py:357
  86.7 41.8 %all-reduce.22 = (bf16[768]{0:T(1024)(128)(2,1)S(1)}, bf16[768]{0:T(1024)(128)(2,1)S(1)}, bf16[3072]{0:T(1024)(128)(2,1)S(1)}, bf16[768]{0:T(1024)(128)(2,1)S(1)...) all-reduce(bf16[768]{0:T(1024)(128)(2,1)S(1)} %dynamic-update-slice, ...), channel_id=1, replica_groups=mesh['dp'=8,'seq'=4] {'dp','seq'}, use_global_device_ids=true, to_apply=%add.9 | all-reduce | flops 6912 | bytes 27648
  140.2 3.2 collective-permute-start.5
  153.3 23.5 %all-gather.12.cloned.1.call-done = bf16[768,768]{1,0:T(8,128)(2,1)} async-done(((bf16[24,768]{1,0:T(8,128)(2,1)}), bf16[768,768]{1,0:T(8,128)(2,1)}) %all-gather.12.cloned.1.call-update) | async-done | bytes 1179664 | tf_op jit(solution)/shard_map/all_gather | solution.py:353
  176.8 3.2 convolution_convert_fusion.5
  181.6 3.8 collective-permute-start
  195.6 3.9 reshape.505
  205.2 3.9 reshape.500
  211.1 10.7 multiply_reduce_fusion.5
  223.7 3.9 collective-permute-start.3
  230.4 4.3 collective-permute-start.7
  250.2 7.1 fusion
  257.3 5.5 fusion.1
  268.8 4.3 fusion.23
  273.2 3.8 fusion.3
  279.0 4.7 fusion.66
  285.1 3.9 fusion.50
  290.1 3.4 fusion.142
  299.5 6.5 fusion.5
  307.2 4.2 fusion.62
  312.7 3.7 fusion.53
  319.8 4.8 fusion.104
  327.3 35.0 %multiply_convert_fusion.3 = (bf16[512,3072]{1,0:T(8,128)(2,1)}, f32[512,3072]{1,0:T(8,128)}, bf16[512,3072]{1,0:T(8,128)(2,1)}, f32[512,3072]{1,0:T(8,128)}, f32[512,3072]{1,0:T(8,128)}) fusion(f32[3072]{0:T(1024)S(1)} %copy-done.127, f32[512,3072]{1,0:T(8,128)S(1)} %fusion.104, bf16[768,3072]{1,0:T(8,128)(2,1)S(1)} %copy-done.139, ...), kind=kOutput, calls=%fused_computation.41 | convolution fusion | flops 2625503232 | bytes 37771264 | tf_op jit(solution)/shard_map/dot_general | solution.py:168
  364.5 6.2 fusion.145
  381.1 4.9 fusion.149
  386.1 18.2 %convert_reduce_fusion.1 = (f32[3072]{0:T(1024)}, bf16[512,3072]{1,0:T(8,128)(2,1)}, f32[3072]{0:T(1024)}, bf16[512,3072]{1,0:T(8,128)(2,1)}) fusion(f32[512,3072]{1,0:T(8,128)} %get-tuple-element.159, f32[512,3072]{1,0:T(8,128)} %get-tuple-element.234, f32[3072]{0:T(1024)S(1)} %copy-done.127, f32[512,3072]{1,0:T(8,128)} %fusion.149, ...), kind=kOutput, calls=%fused_computation.19 | convolution fusion | flops 2469390336 | bytes 43290624 | tf_op jit(solution)/shard_map/dot_general | solution.py:58
  404.2 6.5 add_add_fusion.6
  410.8 6.5 multiply_reduce_fusion.9
  427.1 5.3 fusion.60
  433.2 7.1 multiply_reduce_fusion
  440.4 4.4 multiply_reduce_fusion.6
  451.9 5.3 fusion.64
  458.0 6.2 multiply_reduce_fusion.1
  469.7 4.5 fusion.30
  496.3 3.4 collective-permute-start.13
  508.3 3.2 collective-permute-start.8
  516.6 9.9 multiply_convert_fusion
  526.6 6.8 multiply_convert_fusion.1
  542.6 4.2 fusion.34
  552.1 3.2 copy.280
  558.4 3.1 copy.269
  565.6 3.2 copy.289
  570.2 4.2 multiply_reduce_fusion.2
  587.4 5.0 reshape.514
  592.3 5.0 reshape.513
  597.3 6.5 fusion.122
  603.9 3.9 collective-permute-start.14
  612.7 5.0 reshape.510
  617.7 4.9 reshape.509
  622.6 4.6 fusion.118
  627.3 4.1 collective-permute-start.10
  635.9 4.1 collective-permute-done.10
  643.2 4.5 fusion.27
  652.7 3.2 copy.293
  660.3 3.2 copy.291
  663.6 4.8 fusion.156
  668.4 5.4 convolution_add_fusion
  674.5 5.4 fusion.106
  680.0 5.7 convolution_add_fusion.1
  694.4 40.5 %all-reduce.21 = (f32[10,768]{1,0:T(8,128)S(1)}, f32[768]{0:T(1024)S(1)}, f32[768]{0:T(1024)S(1)}, f32[3072]{0:T(1024)S(1)}, f32[768]{0:T(1024)S(1)}, /*index=5*/f32[768]{0:T(1024)S(1)}, f32[768]{0:T(1024)S(1)}) all-reduce(f32[10,768]{1,0:T(8,128)S(1)} %add.439, ...), channel_id=6, replica_groups=mesh['dp'=8,'seq'=4] {'dp','seq'}, use_global_device_ids=true, to_apply=%region_42.43.clone | all-reduce | flops 14592 | bytes 116736
  746.4 78.0 %reduce-scatter.24.cloned.1.call-done = f32[24,768]{1,0:T(8,128)} async-done(((f32[768,768]{1,0:T(8,128)}), f32[24,768]{1,0:T(8,128)}) %reduce-scatter.24.cloned.1.call-update) | async-done | bytes 73744
  824.4 104.6 %reduce-scatter.22.cloned.1.call-done = f32[24,768]{1,0:T(8,128)} async-done(((f32[768,768]{1,0:T(8,128)}), f32[24,768]{1,0:T(8,128)}) %reduce-scatter.22.cloned.1.call-update) | async-done | bytes 73744
  929.0 141.1 %reduce-scatter.18.cloned.1.call-done = f32[96,768]{1,0:T(8,128)} async-done(((f32[3072,768]{1,0:T(8,128)}), f32[96,768]{1,0:T(8,128)}) %reduce-scatter.18.cloned.1.call-update) | async-done | bytes 294928 | tf_op jit(solution)/shard_map/reduce_scatter | solution.py:390
  1070.1 142.0 %reduce-scatter.16.cloned.1.call-done = f32[24,3072]{1,0:T(8,128)} async-done(((f32[768,3072]{1,0:T(8,128)}), f32[24,3072]{1,0:T(8,128)}) %reduce-scatter.16.cloned.1.call-update) | async-done | bytes 294928 | tf_op jit(solution)/shard_map/reduce_scatter | solution.py:388
  (640 shorter events, 249.5 us)
Async XLA Ops:
  7.2 78.1 %copy-start.146 = (bf16[24]{0:T(256)(128)(2,1)S(1)}, bf16[24]{0:T(256)(128)(2,1)}, u32[]{:S(2)}) copy-start(bf16[24]{0:T(256)(128)(2,1)} %param.23) | copy-start | bytes 148
  7.2 78.3 %copy-start.147 = (bf16[24]{0:T(256)(128)(2,1)S(1)}, bf16[24]{0:T(256)(128)(2,1)}, u32[]{:S(2)}) copy-start(bf16[24]{0:T(256)(128)(2,1)} %param.24) | copy-start | bytes 148
  7.2 78.5 %copy-start.148 = (bf16[24]{0:T(256)(128)(2,1)S(1)}, bf16[24]{0:T(256)(128)(2,1)}, u32[]{:S(2)}) copy-start(bf16[24]{0:T(256)(128)(2,1)} %param.28) | copy-start | bytes 148
  7.2 78.7 %copy-start.149 = (bf16[24]{0:T(256)(128)(2,1)S(1)}, bf16[24]{0:T(256)(128)(2,1)}, u32[]{:S(2)}) copy-start(bf16[24]{0:T(256)(128)(2,1)} %param.29) | copy-start | bytes 148
  7.2 79.0 %copy-start.150 = (bf16[24]{0:T(256)(128)(2,1)S(1)}, bf16[24]{0:T(256)(128)(2,1)}, u32[]{:S(2)}) copy-start(bf16[24]{0:T(256)(128)(2,1)} %param.30) | copy-start | bytes 148
  7.2 79.2 %copy-start.151 = (bf16[96]{0:T(256)(128)(2,1)S(1)}, bf16[96]{0:T(256)(128)(2,1)}, u32[]{:S(2)}) copy-start(bf16[96]{0:T(256)(128)(2,1)} %param.26) | copy-start | bytes 580
  7.3 125.6 %all-gather.8.cloned.1.call-start = ((), (), s32[]{:S(2)}) async-start(), calls=%async_computation.6 | async-start | bytes 1216512 | tf_op jit(solution)/shard_map/all_gather | solution.py:354
  8.0 128.1 %all-gather.10.cloned.1.call-start = ((), (), s32[]{:S(2)}) async-start(), calls=%async_computation.7 | async-start | bytes 1216512 | tf_op jit(solution)/shard_map/all_gather | solution.py:355
  8.7 168.0 %all-gather.12.cloned.1.call-start = ((), (), s32[]{:S(2)}) async-start(), calls=%async_computation.8 | async-start | bytes 1216512 | tf_op jit(solution)/shard_map/all_gather | solution.py:353
  9.5 280.5 %all-gather.14.cloned.1.call-start = ((), (), s32[]{:S(2)}) async-start(), calls=%async_computation.9 | async-start | bytes 1216512 | tf_op jit(solution)/shard_map/all_gather | solution.py:356
  10.0 309.7 %all-gather.16.cloned.1.call-start = ((), (), s32[]{:S(2)}) async-start(), calls=%async_computation.10 | async-start | bytes 4866048 | tf_op jit(solution)/shard_map/all_gather | solution.py:360
  10.6 353.8 %all-gather.18.cloned.1.call-start = ((), (), s32[]{:S(2)}) async-start(), calls=%async_computation.11 | async-start | bytes 4866048 | tf_op jit(solution)/shard_map/all_gather | solution.py:362
  11.2 735.2 %reduce-scatter.14.cloned.1.call-start = ((), (), s32[]{:S(2)}) async-start(), calls=%async_computation.12 | async-start | bytes 2433024 | tf_op jit(solution)/shard_map/reduce_scatter | solution.py:384
  18.1 299.3 %copy-start.16 = (bf16[2,256,768]{2,1,0:T(8,128)(2,1)}, bf16[2,256,768]{2,1,0:T(8,128)(2,1)S(1)}, u32[]{:S(2)}) copy-start(bf16[2,256,768]{2,1,0:T(8,128)(2,1)S(1)} %get-tuple-element.184) | copy-start | bytes 2359300
  84.2 126.9 %copy-start.89 = (f32[2,5,768]{2,1,0:T(8,128)}, f32[2,5,768]{2,1,0:T(8,128)S(1)}, u32[]{:S(2)}) copy-start(f32[2,5,768]{2,1,0:T(8,128)S(1)} %reshape.516) | copy-start | bytes 92164
  132.9 174.3 %copy-start.71 = (pred[2,256,192]{1,2,0:T(8,128)(4,1)}, pred[2,256,192]{1,2,0:T(8,128)(4,1)S(1)}, u32[]{:S(2)}) copy-start(pred[2,256,192]{1,2,0:T(8,128)(4,1)S(1)} %get-tuple-element.200) | copy-start | bytes 294916
  140.2 52.7 %collective-permute-start.5 = (bf16[2,2,64,768]{3,2,1,0:T(8,128)(2,1)}, bf16[2,2,64,768]{3,2,1,0:T(8,128)(2,1)}, u32[]{:S(2)}, u32[]{:S(2)}) collective-permute-start(bf16[2,2,64,768]{3,2,1,0:T(8,128)(2,1)} %get-tuple-element.182), channel_id=1, source_target_pairs={{1,0},{2,1},{3,2},{5,4},{6,5},{7,6},{9,8},{10,9},{11,10},{13,12},{... | collective-permute-start | bytes 1179656 | tf_op jit(solution)/shard_map/ppermute | solution.py:26
  149.2 30.8 %copy-start.21 = (bf16[512,768]{1,0:T(8,128)(2,1)}, bf16[512,768]{1,0:T(8,128)(2,1)S(1)}, u32[]{:S(2)}) copy-start(bf16[512,768]{1,0:T(8,128)(2,1)S(1)} %convolution_convert_fusion.6) | copy-start | bytes 2359300
  151.3 51.0 %collective-permute-start.1 = (bf16[2,2,64,768]{3,2,1,0:T(8,128)(2,1)}, bf16[2,2,64,768]{3,2,1,0:T(8,128)(2,1)}, u32[]{:S(2)}, u32[]{:S(2)}) collective-permute-start(bf16[2,2,64,768]{3,2,1,0:T(8,128)(2,1)} %get-tuple-element.180), channel_id=1, source_target_pairs={{1,0},{2,1},{3,2},{5,4},{6,5},{7,6},{9,8},{10,9},{11,10},{13,12},{... | collective-permute-start | bytes 1179656 | tf_op jit(solution)/shard_map/ppermute | solution.py:26
  181.6 85.0 %copy-start.3 = (bf16[2,256,12,64]{1,0,3,2:T(2,128)(2,1)}, bf16[2,256,12,64]{1,0,3,2:T(2,128)(2,1)S(1)}, u32[]{:S(2)}) copy-start(bf16[2,256,12,64]{1,0,3,2:T(2,128)(2,1)S(1)} %reshape.499) | copy-start | bytes 2359300
  181.6 48.8 %collective-permute-start = (bf16[2,2,64,768]{3,2,1,0:T(8,128)(2,1)}, bf16[2,2,64,768]{3,2,1,0:T(8,128)(2,1)}, u32[]{:S(2)}, u32[]{:S(2)}) collective-permute-start(bf16[2,2,64,768]{3,2,1,0:T(8,128)(2,1)} %get-tuple-element.179), channel_id=1, source_target_pairs={{0,1},{1,2},{2,3},{4,5},{5,6},{6,7},{8,9},{9,10},{10,11},{12,13},{... | collective-permute-start | bytes 1179656 | tf_op jit(solution)/shard_map/ppermute | solution.py:24
  190.8 106.5 %copy-start.5 = (bf16[2,256,12,64]{1,0,3,2:T(2,128)(2,1)}, bf16[2,256,12,64]{1,0,3,2:T(2,128)(2,1)S(1)}, u32[]{:S(2)}) copy-start(bf16[2,256,12,64]{1,0,3,2:T(2,128)(2,1)S(1)} %reshape.504) | copy-start | bytes 2359300
  190.8 51.5 %collective-permute-start.4 = (bf16[2,2,64,768]{3,2,1,0:T(8,128)(2,1)}, bf16[2,2,64,768]{3,2,1,0:T(8,128)(2,1)}, u32[]{:S(2)}, u32[]{:S(2)}) collective-permute-start(bf16[2,2,64,768]{3,2,1,0:T(8,128)(2,1)} %get-tuple-element.181), channel_id=1, source_target_pairs={{0,1},{1,2},{2,3},{4,5},{5,6},{6,7},{8,9},{9,10},{10,11},{12,13},{... | collective-permute-start | bytes 1179656 | tf_op jit(solution)/shard_map/ppermute | solution.py:24
  211.1 19.3 %copy-start.39 = (bf16[2,2,64,1,768]{4,3,2,1,0:T(2,128)(2,1)}, bf16[2,2,64,1,768]{4,3,2,1,0:T(2,128)(2,1)S(1)}, u32[]{:S(2)}) copy-start(bf16[2,2,64,1,768]{4,3,2,1,0:T(2,128)(2,1)S(1)} %slice.251) | copy-start | bytes 1179652
  211.1 23.6 %copy-start.20 = (bf16[512,768]{1,0:T(8,128)(2,1)S(1)}, bf16[512,768]{1,0:T(8,128)(2,1)}, u32[]{:S(2)}) copy-start(bf16[512,768]{1,0:T(8,128)(2,1)} %copy-done.19) | copy-start | bytes 2359300
  211.1 23.6 %copy-start.22 = (bf16[512,768]{1,0:T(8,128)(2,1)S(1)}, bf16[512,768]{1,0:T(8,128)(2,1)}, u32[]{:S(2)}) copy-start(bf16[512,768]{1,0:T(8,128)(2,1)} %copy-done.21) | copy-start | bytes 2359300
  221.8 41.0 %collective-permute-start.2 = (bf16[2,2,64,768]{3,2,1,0:T(8,128)(2,1)}, bf16[2,2,64,768]{3,2,1,0:T(8,128)(2,1)}, u32[]{:S(2)}, u32[]{:S(2)}) collective-permute-start(bf16[2,2,64,768]{3,2,1,0:T(8,128)(2,1)} %get-tuple-element.119), channel_id=1, source_target_pairs={{0,1},{1,2},{2,3},{4,5},{5,6},{6,7},{8,9},{9,10},{10,11},{12,13},{... | collective-permute-start | bytes 1179656 | tf_op jit(solution)/shard_map/ppermute | solution.py:24
  223.7 39.1 %collective-permute-start.3 = (bf16[2,2,64,768]{3,2,1,0:T(8,128)(2,1)}, bf16[2,2,64,768]{3,2,1,0:T(8,128)(2,1)}, u32[]{:S(2)}, u32[]{:S(2)}) collective-permute-start(bf16[2,2,64,768]{3,2,1,0:T(8,128)(2,1)} %get-tuple-element.119), channel_id=1, source_target_pairs={{1,0},{2,1},{3,2},{5,4},{6,5},{7,6},{9,8},{10,9},{11,10},{13,12},{... | collective-permute-start | bytes 1179656 | tf_op jit(solution)/shard_map/ppermute | solution.py:26
  227.7 65.8 %collective-permute-start.6 = (bf16[2,2,64,768]{3,2,1,0:T(8,128)(2,1)}, bf16[2,2,64,768]{3,2,1,0:T(8,128)(2,1)}, u32[]{:S(2)}, u32[]{:S(2)}) collective-permute-start(bf16[2,2,64,768]{3,2,1,0:T(8,128)(2,1)} %get-tuple-element.120), channel_id=1, source_target_pairs={{0,1},{1,2},{2,3},{4,5},{5,6},{6,7},{8,9},{9,10},{10,11},{12,13},{... | collective-permute-start | bytes 1179656 | tf_op jit(solution)/shard_map/ppermute | solution.py:24
  230.4 63.1 %collective-permute-start.7 = (bf16[2,2,64,768]{3,2,1,0:T(8,128)(2,1)}, bf16[2,2,64,768]{3,2,1,0:T(8,128)(2,1)}, u32[]{:S(2)}, u32[]{:S(2)}) collective-permute-start(bf16[2,2,64,768]{3,2,1,0:T(8,128)(2,1)} %get-tuple-element.120), channel_id=1, source_target_pairs={{1,0},{2,1},{3,2},{5,4},{6,5},{7,6},{9,8},{10,9},{11,10},{13,12},{... | collective-permute-start | bytes 1179656 | tf_op jit(solution)/shard_map/ppermute | solution.py:26
  268.8 14.9 %copy-start.83 = (f32[2,12,256]{2,1,0:T(8,128)}, f32[2,12,256]{2,1,0:T(8,128)S(1)}, u32[]{:S(2)}) copy-start(f32[2,12,256]{2,1,0:T(8,128)S(1)} %max.16) | copy-start | bytes 73732
  293.5 123.8 %copy-start.118 = (f32[512]{0:T(512)}, f32[512]{0:T(512)S(1)}, u32[]{:S(2)}) copy-start(f32[512]{0:T(512)S(1)} %broadcast_multiply_fusion.3) | copy-start | bytes 6148
  298.4 13.0 %copy-start.86 = (f32[2,12,256]{2,1,0:T(8,128)}, f32[2,12,256]{2,1,0:T(8,128)S(1)}, u32[]{:S(2)}) copy-start(f32[2,12,256]{2,1,0:T(8,128)S(1)} %max.17) | copy-start | bytes 73732
  299.5 11.9 slice-start.9
  318.6 98.7 %copy-start.7 = (f32[512,768]{1,0:T(8,128)}, f32[512,768]{1,0:T(8,128)S(1)}, u32[]{:S(2)}) copy-start(f32[512,768]{1,0:T(8,128)S(1)} %get-tuple-element.233) | copy-start | bytes 4718596
  318.6 98.7 %copy-start.111 = (f32[512]{0:T(512)}, f32[512]{0:T(512)S(1)}, u32[]{:S(2)}) copy-start(f32[512]{0:T(512)S(1)} %broadcast_multiply_fusion.1) | copy-start | bytes 6148
  319.7 97.7 %copy-start.130 = (f32[512]{0:T(512)}, f32[512]{0:T(512)S(1)}, u32[]{:S(2)}) copy-start(f32[512]{0:T(512)S(1)} %fusion.98) | copy-start | bytes 6148
  319.7 97.7 %copy-start.114 = (f32[512]{0:T(512)}, f32[512]{0:T(512)S(1)}, u32[]{:S(2)}) copy-start(f32[512]{0:T(512)S(1)} %fusion.100) | copy-start | bytes 6148
  327.3 37.2 %copy-start.137 = (f32[768]{0:T(1024)S(1)}, f32[768]{0:T(1024)}, u32[]{:S(2)}) copy-start(f32[768]{0:T(1024)} %convert_element_type.304) | copy-start | bytes 9220
  418.7 48.6 %copy-start.11 = (f32[512,768]{1,0:T(8,128)}, f32[512,768]{1,0:T(8,128)S(1)}, u32[]{:S(2)}) copy-start(f32[512,768]{1,0:T(8,128)S(1)} %get-tuple-element.149) | copy-start | bytes 4718596
  427.1 13.3 %slice-start.20 = ((s8[4718592]{0:T(1024)(128)(4,1)}), s8[4194304]{0:T(1024)(128)(4,1)S(1)}, s32[]{:S(2)}) async-start(s8[4718592]{0:T(1024)(128)(4,1)} %bitcast.235), calls=%async_computation.38 | async-start | bytes 8388608
  444.8 22.5 %copy-start.120 = (f32[512]{0:T(512)}, f32[512]{0:T(512)S(1)}, u32[]{:S(2)}) copy-start(f32[512]{0:T(512)S(1)} %negate_multiply_fusion.4) | copy-start | bytes 6148
  444.9 12.3 %slice-start.3 = ((s8[9437184]{0:T(1024)(128)(4,1)}), s8[1048576]{0:T(1024)(128)(4,1)S(1)}, s32[]{:S(2)}) async-start(s8[9437184]{0:T(1024)(128)(4,1)} %bitcast.223), calls=%async_computation.21 | async-start | bytes 2097152
  451.9 12.4 %slice-start.18 = ((s8[4718592]{0:T(1024)(128)(4,1)}), s8[4194304]{0:T(1024)(128)(4,1)S(1)}, s32[]{:S(2)}) async-start(s8[4718592]{0:T(1024)(128)(4,1)} %bitcast.233), calls=%async_computation.36 | async-start | bytes 8388608
  458.0 11.7 slice-start.15
  458.0 11.7 slice-start.16
  467.3 12.5 %slice-start.26 = ((s8[4718592]{0:T(1024)(128)(4,1)}), s8[4194304]{0:T(1024)(128)(4,1)S(1)}, s32[]{:S(2)}) async-start(s8[4718592]{0:T(1024)(128)(4,1)} %bitcast.285), calls=%async_computation.44 | async-start | bytes 8388608
  493.8 75.0 %collective-permute-start.12 = (bf16[2,2,64,768]{3,2,1,0:T(8,128)(2,1)}, bf16[2,2,64,768]{3,2,1,0:T(8,128)(2,1)}, u32[]{:S(2)}, u32[]{:S(2)}) collective-permute-start(bf16[2,2,64,768]{3,2,1,0:T(8,128)(2,1)} %get-tuple-element.187), channel_id=1, source_target_pairs={{0,1},{1,2},{2,3},{4,5},{5,6},{6,7},{8,9},{9,10},{10,11},{12,13},{... | collective-permute-start | bytes 1179656 | tf_op jit(solution)/shard_map/ppermute | solution.py:24
  496.3 72.6 %collective-permute-start.13 = (bf16[2,2,64,768]{3,2,1,0:T(8,128)(2,1)}, bf16[2,2,64,768]{3,2,1,0:T(8,128)(2,1)}, u32[]{:S(2)}, u32[]{:S(2)}) collective-permute-start(bf16[2,2,64,768]{3,2,1,0:T(8,128)(2,1)} %get-tuple-element.188), channel_id=1, source_target_pairs={{1,0},{2,1},{3,2},{5,4},{6,5},{7,6},{9,8},{10,9},{11,10},{13,12},{... | collective-permute-start | bytes 1179656 | tf_op jit(solution)/shard_map/ppermute | solution.py:26
  508.3 69.2 %collective-permute-start.8 = (bf16[2,2,64,768]{3,2,1,0:T(8,128)(2,1)}, bf16[2,2,64,768]{3,2,1,0:T(8,128)(2,1)}, u32[]{:S(2)}, u32[]{:S(2)}) collective-permute-start(bf16[2,2,64,768]{3,2,1,0:T(8,128)(2,1)} %get-tuple-element.185), channel_id=1, source_target_pairs={{0,1},{1,2},{2,3},{4,5},{5,6},{6,7},{8,9},{9,10},{10,11},{12,13},{... | collective-permute-start | bytes 1179656 | tf_op jit(solution)/shard_map/ppermute | solution.py:24
  511.5 66.0 %collective-permute-start.9 = (bf16[2,2,64,768]{3,2,1,0:T(8,128)(2,1)}, bf16[2,2,64,768]{3,2,1,0:T(8,128)(2,1)}, u32[]{:S(2)}, u32[]{:S(2)}) collective-permute-start(bf16[2,2,64,768]{3,2,1,0:T(8,128)(2,1)} %get-tuple-element.186), channel_id=1, source_target_pairs={{1,0},{2,1},{3,2},{5,4},{6,5},{7,6},{9,8},{10,9},{11,10},{13,12},{... | collective-permute-start | bytes 1179656 | tf_op jit(solution)/shard_map/ppermute | solution.py:26
  514.2 12.3 %slice-start.6 = ((s8[9437184]{0:T(1024)(128)(4,1)}), s8[1048576]{0:T(1024)(128)(4,1)S(1)}, s32[]{:S(2)}) async-start(s8[9437184]{0:T(1024)(128)(4,1)} %bitcast.225), calls=%async_computation.24 | async-start | bytes 2097152
  516.6 229.8 %reduce-scatter.20.cloned.1.call-start = ((), (), s32[]{:S(2)}) async-start(), calls=%async_computation.15 | async-start | bytes 2433024
  568.8 255.6 %reduce-scatter.24.cloned.1.call-start = ((), (), s32[]{:S(2)}) async-start(), calls=%async_computation.17 | async-start | bytes 2433024
  603.9 30.5 %collective-permute-start.14 = (bf16[2,2,64,768]{3,2,1,0:T(8,128)(2,1)S(1)}, bf16[2,2,64,768]{3,2,1,0:T(8,128)(2,1)}, u32[]{:S(2)}, u32[]{:S(2)}) collective-permute-start(bf16[2,2,64,768]{3,2,1,0:T(8,128)(2,1)S(1)} %get-tuple-element.164), channel_id=1, source_target_pairs={{0,1},{1,2},{2,3},{4,5},{5,6},{6,7},{8,9},{9,10},{10,11},{12,13},{... | collective-permute-start | bytes 1179656 | tf_op jit(solution)/shard_map/ppermute | solution.py:24
  607.8 26.6 %collective-permute-start.15 = (bf16[2,2,64,768]{3,2,1,0:T(8,128)(2,1)S(1)}, bf16[2,2,64,768]{3,2,1,0:T(8,128)(2,1)}, u32[]{:S(2)}, u32[]{:S(2)}) collective-permute-start(bf16[2,2,64,768]{3,2,1,0:T(8,128)(2,1)S(1)} %get-tuple-element.165), channel_id=1, source_target_pairs={{1,0},{2,1},{3,2},{5,4},{6,5},{7,6},{9,8},{10,9},{11,10},{13,12},{... | collective-permute-start | bytes 1179656 | tf_op jit(solution)/shard_map/ppermute | solution.py:26
  627.2 15.9 %slice-start.24 = ((s8[4718592]{0:T(1024)(128)(4,1)}), s8[4194304]{0:T(1024)(128)(4,1)S(1)}, s32[]{:S(2)}) async-start(s8[4718592]{0:T(1024)(128)(4,1)} %bitcast.239), calls=%async_computation.42 | async-start | bytes 8388608
  627.3 12.7 %collective-permute-start.10 = (bf16[2,2,64,768]{3,2,1,0:T(8,128)(2,1)S(1)}, bf16[2,2,64,768]{3,2,1,0:T(8,128)(2,1)S(1)}, u32[]{:S(2)}, u32[]{:S(2)}) collective-permute-start(bf16[2,2,64,768]{3,2,1,0:T(8,128)(2,1)S(1)} %get-tuple-element.162), channel_id=1, source_target_pairs={{0,1},{1,2},{2,3},{4,5},{5,6},{6,7},{8,9},{9,10},{10,11},{12,13},{... | collective-permute-start | bytes 1179656 | tf_op jit(solution)/shard_map/ppermute | solution.py:24
  631.5 11.4 collective-permute-start.11
  655.9 273.1 %reduce-scatter.22.cloned.1.call-start = ((), (), s32[]{:S(2)}) async-start(), calls=%async_computation.16 | async-start | bytes 2433024
  663.5 406.5 %reduce-scatter.18.cloned.1.call-start = ((), (), s32[]{:S(2)}) async-start(), calls=%async_computation.14 | async-start | bytes 9732096 | tf_op jit(solution)/shard_map/reduce_scatter | solution.py:390
  673.9 538.2 %reduce-scatter.16.cloned.1.call-start = ((), (), s32[]{:S(2)}) async-start(), calls=%async_computation.13 | async-start | bytes 9732096 | tf_op jit(solution)/shard_map/reduce_scatter | solution.py:388
  690.4 48.7 %copy-start.48 = (bf16[1,2,256,768]{3,2,1,0:T(8,128)(2,1)S(1)}, bf16[1,2,256,768]{3,2,1,0:T(8,128)(2,1)}, u32[]{:S(2)}) copy-start(bf16[1,2,256,768]{3,2,1,0:T(8,128)(2,1)} %get-tuple-element.176) | copy-start | bytes 2359300
  694.4 47.0 %copy-start.60 = (bf16[1,2,256,768]{3,2,1,0:T(8,128)(2,1)S(1)}, bf16[1,2,256,768]{3,2,1,0:T(8,128)(2,1)}, u32[]{:S(2)}) copy-start(bf16[1,2,256,768]{3,2,1,0:T(8,128)(2,1)} %get-tuple-element.178) | copy-start | bytes 2359300
  (147 other events, 639.2 us)
Sparse Core Ops, SparseCore 0:
  10.9 53.7 all-gather.7
  67.5 53.1 all-gather.9
  123.6 53.1 all-gather.11
  179.4 53.5 all-gather.13
  235.7 63.6 all-gather.15
  302.0 62.4 all-gather.17
  516.7 98.8 reduce-scatter.13
  622.3 98.1 reduce-scatter.19
  726.3 98.0 reduce-scatter.23
  830.9 97.9 reduce-scatter.21
  935.4 134.5 reduce-scatter.17
  1077.4 134.5 reduce-scatter.15
where the time goes:
time: 1230 us; the launch traced here: 1220 us
  waiting for transfers between devices  502 us (41%)
  matrix products  241 us (20%)
  local copies, waits for them, and re-layouts  150 us (12%)
  blocking collectives  148 us (12%)
  other arithmetic  111 us (9%)
  starting transfers between devices  49.9 us (4%)
  between operations  17.5 us (1%)
    unnamed x15, waiting for transfers between devices  186 us
    reduce_scatter x1, waiting for transfers between devices, local(): lax.psum_scatter(grad_total[7], ('dp', 'seq'), scatter_dimension=0, tiled...  142 us
    reduce_scatter x1, waiting for transfers between devices, local(): lax.psum_scatter(grad_total[9], ('dp', 'seq'), scatter_dimension=0, tiled...  141 us
    unnamed x2, blocking collectives  82.3 us
    all_gather x1, blocking collectives, local(): lax.all_gather(shards[4], ('dp', 'seq'), axis=1, tiled=True)  65.7 us
    dot_general x12, matrix products, dot_right(): lax.dot_general(left, right, (((1,), (1,)), ((), ())), preferred_element_...  48.5 us
    dot_general x2, matrix products, run_micro(): jnp.dot(normed_low, w_inner, preferred_element_type=jnp.float32)  39.8 us
    dot_general x12, matrix products, dot_left(): lax.dot_general(left, right, (((0,), (0,)), ((), ())), preferred_element_...  37.8 us
  transfers between devices with their start and end apart: 28, of which 8 were waited for; matrix products, arithmetic and copies ran while one was open for 30% of the time, Pallas kernels for 0%

commit v1 on v0

v1 whole, which is shorter than its diff:
```python
import functools

import jax
import jax.numpy as jnp
from jax import lax
from jax.experimental import pallas as pl
from jax.experimental.pallas import tpu as pltpu
from jax.sharding import PartitionSpec as P

HEADS = 12
HEAD_DIM = 64
WIN = 128
PWIN = 512
EPS = 1e-05

LANES = 128
QB = 128
HALO = PWIN // 2
PAD = 16
NEAR = QB + WIN
FAR = (QB + PWIN) // 4
KEYS = NEAR + FAR
MASKED = -1e30

F32 = jnp.float32
BF16 = jnp.bfloat16


def nt(left, right):
    return lax.dot_general(left, right, (((1,), (1,)), ((), ())), preferred_element_type=F32)


def tn(left, right):
    return lax.dot_general(left, right, (((0,), (0,)), ((), ())), preferred_element_type=F32)


def nn(left, right):
    return lax.dot_general(left, right, (((1,), (0,)), ((), ())), preferred_element_type=F32)


def slot_taps(wide, slots):
    return [wide[pl.ds(tap, slots, stride=4), :] for tap in range(5)]


def pool(taps, same_ref, w_ref, first):
    total = None
    for tap in range(5):
        term = taps[tap] * same_ref[0, tap] * w_ref[first + tap : first + tap + 1, :]
        total = term if total is None else total + term
    return total.astype(BF16)


def pair_stack(rows):
    lane = lax.broadcasted_iota(jnp.int32, rows.shape, 1)
    zero = jnp.zeros_like(rows)
    return jnp.concatenate(
        (jnp.where(lane < HEAD_DIM, rows, zero), jnp.where(lane < HEAD_DIM, zero, rows)), axis=0
    )


def pair_join(both):
    joined = jnp.concatenate((both[:HEAD_DIM, :QB], both[HEAD_DIM:, QB:]), axis=0)
    return joined.T


def keys_of(ref, pooled, block):
    near = HALO - WIN // 2 + block * QB
    far = block * QB // 4
    return jnp.concatenate((ref[0, near : near + NEAR, :], pooled[far : far + FAR, :]), axis=0)


def scores_of(keys, stacked, bias):
    return nt(keys, stacked) + jnp.concatenate((bias, bias), axis=1)


def attn_fwd_kernel(
    q_ref, k_ref, v_ref, w_ref, same_ref, bias_ref, out_ref, lse_ref, k_wide, v_wide, pk_ref, pv_ref
):
    slots = pk_ref.shape[0]
    k_wide[...] = k_ref[0].astype(F32)
    v_wide[...] = v_ref[0].astype(F32)
    pk_ref[...] = pool(slot_taps(k_wide, slots), same_ref, w_ref, 0)
    pv_ref[...] = pool(slot_taps(v_wide, slots), same_ref, w_ref, 5)
    scale = jnp.asarray(HEAD_DIM**-0.5, BF16)
    for block in range(q_ref.shape[1] // QB):
        rows = slice(block * QB, (block + 1) * QB)
        keys = keys_of(k_ref, pk_ref, block)
        values = keys_of(v_ref, pv_ref, block)
        stacked = pair_stack(q_ref[0, rows, :] * scale)
        scores = scores_of(keys, stacked, bias_ref[0, block])
        top = jnp.max(scores, axis=0, keepdims=True)
        weights = jnp.exp(scores - top)
        denom = jnp.sum(weights, axis=0, keepdims=True)
        probs = (weights * (1.0 / denom)).astype(BF16)
        out_ref[0, rows, :] = pair_join(tn(values, probs)).astype(BF16)
        lse_ref[0, 0, block : block + 1, :] = top + jnp.log(denom)


def attn_bwd_kernel(
    q_ref,
    k_ref,
    v_ref,
    w_ref,
    same_ref,
    bias_ref,
    lse_ref,
    do_ref,
    dq_ref,
    dk_ref,
    dv_ref,
    dw_ref,
    k_wide,
    v_wide,
    pk_ref,
    pv_ref,
    dpk_ref,
    dpv_ref,
):
    slots = pk_ref.shape[0]
    k_wide[...] = k_ref[0].astype(F32)
    v_wide[...] = v_ref[0].astype(F32)
    pk_ref[...] = pool(slot_taps(k_wide, slots), same_ref, w_ref, 0)
    pv_ref[...] = pool(slot_taps(v_wide, slots), same_ref, w_ref, 5)
    dpk_ref[...] = jnp.zeros_like(dpk_ref)
    dpv_ref[...] = jnp.zeros_like(dpv_ref)
    scale = jnp.asarray(HEAD_DIM**-0.5, BF16)
    near_parts = []
    for block in range(q_ref.shape[1] // QB):
        rows = slice(block * QB, (block + 1) * QB)
        keys = keys_of(k_ref, pk_ref, block)
        values = keys_of(v_ref, pv_ref, block)
        stacked = pair_stack(q_ref[0, rows, :] * scale)
        do_stacked = pair_stack(do_ref[0, rows, :])
        probs = jnp.exp(
            scores_of(keys, stacked, bias_ref[0, block]) - lse_ref[0, 0, block : block + 1, :]
        )
        d_probs = nt(values, do_stacked)
        row_dot = jnp.sum(probs * d_probs, axis=0, keepdims=True)
        d_scores = (probs * (d_probs - row_dot)).astype(BF16)
        d_values = nn(probs.astype(BF16), do_stacked)
        d_keys = nn(d_scores, stacked)
        dq_ref[0, rows, :] = (pair_join(tn(keys, d_scores)) * HEAD_DIM**-0.5).astype(BF16)
        far = slice(block * QB // 4, block * QB // 4 + FAR)
        dpk_ref[far, :] += d_keys[NEAR:]
        dpv_ref[far, :] += d_values[NEAR:]
        near_parts.append((d_keys[:NEAR], d_values[:NEAR]))
    sides = ((k_wide, dpk_ref, dk_ref, 0), (v_wide, dpv_ref, dv_ref, 1))
    for wide, d_pool_ref, out_ref, side in sides:
        d_pool = d_pool_ref[...]
        taps = slot_taps(wide, slots)
        masked = [d_pool * same_ref[0, tap] for tap in range(5)]
        for tap in range(5):
            row = 5 * side + tap
            dw_ref[0, row : row + 1, :] = jnp.sum(masked[tap] * taps[tap], axis=0, keepdims=True)
        spread = [masked[tap] * w_ref[5 * side + tap : 5 * side + tap + 1, :] for tap in range(5)]
        wide[4 * slots :, :] = jnp.zeros((wide.shape[0] - 4 * slots, LANES), F32)
        for tap in range(4):
            wide[pl.ds(tap, slots, stride=4), :] = spread[tap]
        wide[pl.ds(4, slots, stride=4), :] += spread[4]
        for block, parts in enumerate(near_parts):
            near = HALO - WIN // 2 + block * QB
            wide[near : near + NEAR, :] += parts[side]
        out_ref[0] = wide[...].astype(BF16)
    dw_ref[0, 10:, :] = jnp.zeros((dw_ref.shape[1] - 10, LANES), F32)


def attention_specs(ext, group, slots):
    return [
        pl.BlockSpec((1, group, LANES), lambda s, p: (s, 0, p)),
        pl.BlockSpec((1, ext, LANES), lambda s, p: (s, 0, p)),
        pl.BlockSpec((1, ext, LANES), lambda s, p: (s, 0, p)),
        pl.BlockSpec((16, LANES), lambda s, p: (0, p)),
        pl.BlockSpec((1, 5, slots, LANES), lambda s, p: (s, 0, 0, 0)),
        pl.BlockSpec((1, group // QB, KEYS, LANES), lambda s, p: (s, 0, 0, 0)),
    ]


def attention_forward(queries, keys, values, taps, same, bias):
    seqs, group, width = queries.shape
    ext = keys.shape[1]
    slots = same.shape[2]
    pairs = width // LANES
    blocks = group // QB
    wide = pltpu.VMEM((ext, LANES), F32)
    pooled = pltpu.VMEM((slots, LANES), BF16)
    return pl.pallas_call(
        attn_fwd_kernel,
        grid=(seqs, pairs),
        in_specs=attention_specs(ext, group, slots),
        out_specs=[
            pl.BlockSpec((1, group, LANES), lambda s, p: (s, 0, p)),
            pl.BlockSpec((1, 1, blocks, 2 * QB), lambda s, p: (s, p, 0, 0)),
        ],
        out_shape=[
            jax.ShapeDtypeStruct((seqs, group, width), BF16),
            jax.ShapeDtypeStruct((seqs, pairs, blocks, 2 * QB), F32),
        ],
        scratch_shapes=[wide, wide, pooled, pooled],
        compiler_params=pltpu.CompilerParams(vmem_limit_bytes=32 << 20),
        cost_estimate=pl.CostEstimate(
            flops=seqs * HEADS * blocks * QB * KEYS * LANES * 8,
            bytes_accessed=seqs * width * (ext * 4 + group * 4),
            transcendentals=seqs * HEADS * group * KEYS,
        ),
        name="attn_fwd",
    )(queries, keys, values, taps, same, bias)


def attention_backward(queries, keys, values, taps, same, bias, lse, d_mixed):
    seqs, group, width = queries.shape
    ext = keys.shape[1]
    slots = same.shape[2]
    pairs = width // LANES
    blocks = group // QB
    wide = pltpu.VMEM((ext, LANES), F32)
    pooled = pltpu.VMEM((slots, LANES), BF16)
    d_pooled = pltpu.VMEM((slots, LANES), F32)
    own = pl.BlockSpec((1, group, LANES), lambda s, p: (s, 0, p))
    extended = pl.BlockSpec((1, ext, LANES), lambda s, p: (s, 0, p))
    return pl.pallas_call(
        attn_bwd_kernel,
        grid=(seqs, pairs),
        in_specs=attention_specs(ext, group, slots)
        + [pl.BlockSpec((1, 1, blocks, 2 * QB), lambda s, p: (s, p, 0, 0)), own],
        out_specs=[
            own,
            extended,
            extended,
            pl.BlockSpec((1, 16, LANES), lambda s, p: (s, 0, p)),
        ],
        out_shape=[
            jax.ShapeDtypeStruct((seqs, group, width), BF16),
            jax.ShapeDtypeStruct((seqs, ext, width), BF16),
            jax.ShapeDtypeStruct((seqs, ext, width), BF16),
            jax.ShapeDtypeStruct((seqs, 16, width), F32),
        ],
        scratch_shapes=[wide, wide, pooled, pooled, d_pooled, d_pooled],
        compiler_params=pltpu.CompilerParams(vmem_limit_bytes=32 << 20),
        cost_estimate=pl.CostEstimate(
            flops=seqs * HEADS * blocks * QB * KEYS * LANES * 20,
            bytes_accessed=seqs * width * (ext * 8 + group * 6),
            transcendentals=seqs * HEADS * group * KEYS,
        ),
        name="attn_bwd",
    )(queries, keys, values, taps, same, bias, lse, d_mixed)


ROWS = 256
HALF_PI = 0.3989422804014327


def row_sum(value):
    return jnp.sum(value, axis=0, keepdims=True)


def row_mean(value):
    return jnp.mean(value, axis=1, keepdims=True)


def normalize(value):
    centered = value - row_mean(value)
    inv = lax.rsqrt(row_mean(centered * centered) + EPS)
    return centered * inv, inv


def normalize_back(grad, normed, inv):
    return inv * (grad - row_mean(grad) - normed * row_mean(grad * normed))


def ffn_kernel(
    panels,
    x_ref,
    mixed_ref,
    cot_ref,
    wo_ref,
    small_ref,
    bias_ref,
    w_in_ref,
    w_out_ref,
    y_ref,
    d_first_ref,
    d_mixed_ref,
    d_wo_ref,
    d_small_ref,
    d_bias_ref,
    d_in_ref,
    d_out_ref,
    n_one,
    inv_one,
    low,
    hidden,
    slope,
    acc,
    d_outer,
    d_inner,
):
    step = pl.program_id(0)
    tokens, width = x_ref.shape
    chunks = tokens // ROWS
    gain_one, shift_one, outer_bias, gain_two, shift_two = (
        small_ref[i : i + 1, :] for i in range(5)
    )

    @pl.when(step == 0)
    def _():
        def body(i, carry):
            rows = pl.ds(pl.multiple_of(i * ROWS, ROWS), ROWS)
            first = x_ref[rows, :].astype(F32) + nn(mixed_ref[rows, :], wo_ref[...])
            normed, inv = normalize(first)
            n_one[rows, :] = normed
            inv_one[rows, :] = jnp.broadcast_to(inv, (ROWS, LANES))
            out = normed * gain_one + shift_one
            low[rows, :] = out.astype(BF16)
            acc[rows, :] = out + outer_bias
            return carry

        lax.fori_loop(0, chunks, body, 0)

    @pl.when(step < panels)
    def _():
        def body(i, carry):
            rows = pl.ds(pl.multiple_of(i * ROWS, ROWS), ROWS)
            inner = nn(low[rows, :], w_in_ref[0]) + bias_ref[0]
            cdf = 0.5 * (1.0 + lax.erf(inner * 0.7071067811865476))
            pdf = HALF_PI * jnp.exp(-0.5 * inner * inner)
            out = (inner * cdf).astype(BF16)
            hidden[step, rows, :] = out
            slope[step, rows, :] = cdf + inner * pdf
            acc[rows, :] += nn(out, w_out_ref[0])
            return carry

        lax.fori_loop(0, chunks, body, 0)

    @pl.when(step == panels)
    def _():
        def body(i, carry):
            d_gain, d_shift, d_bias = carry
            rows = pl.ds(pl.multiple_of(i * ROWS, ROWS), ROWS)
            normed, inv = normalize(acc[rows, :])
            y_ref[rows, :] = (normed * gain_two + shift_two).astype(BF16)
            grad = cot_ref[rows, :].astype(F32)
            d_second = normalize_back(grad * gain_two, normed, inv)
            low_grad = d_second.astype(BF16)
            acc[rows, :] = d_second
            d_outer[rows, :] = low_grad
            return (
                d_gain + row_sum(grad * normed),
                d_shift + row_sum(grad),
                d_bias + row_sum(low_grad.astype(F32)),
            )

        zero = jnp.zeros((1, width), F32)
        d_gain, d_shift, d_bias = lax.fori_loop(0, chunks, body, (zero, zero, zero))
        d_small_ref[2:3, :] = d_bias
        d_small_ref[3:4, :] = d_gain
        d_small_ref[4:5, :] = d_shift
        d_small_ref[5:, :] = jnp.zeros((3, width), F32)

    @pl.when(step >= panels)
    def _():
        panel = step - panels

        def body(i, d_bias):
            rows = pl.ds(pl.multiple_of(i * ROWS, ROWS), ROWS)
            d_hidden = nt(d_outer[rows, :], w_out_ref[0])
            grad = (d_hidden * slope[panel, rows, :]).astype(BF16)
            d_inner[rows, :] = grad
            acc[rows, :] += nt(grad, w_in_ref[0])
            return d_bias + row_sum(grad.astype(F32))

        d_bias_ref[0] = lax.fori_loop(0, chunks, body, jnp.zeros(d_bias_ref.shape[1:], F32))
        d_out_ref[0] = tn(hidden[panel], d_outer[...]).astype(BF16)
        d_in_ref[0] = tn(low[...], d_inner[...]).astype(BF16)

    @pl.when(step == 2 * panels - 1)
    def _():
        def body(i, carry):
            d_gain, d_shift = carry
            rows = pl.ds(pl.multiple_of(i * ROWS, ROWS), ROWS)
            grad = acc[rows, :]
            normed = n_one[rows, :]
            d_first = normalize_back(grad * gain_one, normed, inv_one[rows, 0:1])
            d_first_ref[rows, :] = d_first
            low_grad = d_first.astype(BF16)
            d_outer[rows, :] = low_grad
            d_mixed_ref[rows, :] = nt(low_grad, wo_ref[...]).astype(BF16)
            return d_gain + row_sum(grad * normed), d_shift + row_sum(grad)

        zero = jnp.zeros((1, width), F32)
        d_gain, d_shift = lax.fori_loop(0, chunks, body, (zero, zero))
        d_small_ref[0:1, :] = d_gain
        d_small_ref[1:2, :] = d_shift
        d_wo_ref[...] = tn(mixed_ref[...], d_outer[...]).astype(BF16)


def feed_forward(x, mixed, cot, wo, small, bias, w_in, w_out):
    tokens, width = x.shape
    panels, _, panel = w_in.shape

    def whole(*shape):
        return pl.BlockSpec(
            shape, lambda j: (0,) * len(shape), pipeline_mode=pl.Buffered(buffer_count=1)
        )

    def now(j):
        return (lax.rem(j, panels), 0, 0)

    def later(j):
        return (jnp.maximum(j - panels, 0), 0, 0)

    weight = pl.BlockSpec((1, width, panel), now)
    weight_out = pl.BlockSpec((1, panel, width), now)
    return pl.pallas_call(
        functools.partial(ffn_kernel, panels),
        grid=(2 * panels,),
        in_specs=[
            whole(tokens, width),
            whole(tokens, width),
            whole(tokens, width),
            whole(width, width),
            whole(8, width),
            pl.BlockSpec((1, 1, panel), now),
            weight,
            weight_out,
        ],
        out_specs=[
            whole(tokens, width),
            whole(tokens, width),
            whole(tokens, width),
            whole(width, width),
            whole(8, width),
            pl.BlockSpec((1, 1, panel), later),
            pl.BlockSpec((1, width, panel), later),
            pl.BlockSpec((1, panel, width), later),
        ],
        out_shape=[
            jax.ShapeDtypeStruct((tokens, width), BF16),
            jax.ShapeDtypeStruct((tokens, width), F32),
            jax.ShapeDtypeStruct((tokens, width), BF16),
            jax.ShapeDtypeStruct((width, width), BF16),
            jax.ShapeDtypeStruct((8, width), F32),
            jax.ShapeDtypeStruct((panels, 1, panel), F32),
            jax.ShapeDtypeStruct((panels, width, panel), BF16),
            jax.ShapeDtypeStruct((panels, panel, width), BF16),
        ],
        scratch_shapes=[
            pltpu.VMEM((tokens, width), F32),
            pltpu.VMEM((tokens, LANES), F32),
            pltpu.VMEM((tokens, width), BF16),
            pltpu.VMEM((panels, tokens, panel), BF16),
            pltpu.VMEM((panels, tokens, panel), F32),
            pltpu.VMEM((tokens, width), F32),
            pltpu.VMEM((tokens, width), BF16),
            pltpu.VMEM((tokens, panel), BF16),
        ],
        compiler_params=pltpu.CompilerParams(vmem_limit_bytes=60 << 20),
        cost_estimate=pl.CostEstimate(
            flops=2 * tokens * width * (6 * panels * panel + 3 * width),
            bytes_accessed=8 * panels * panel * width + 16 * tokens * width,
            transcendentals=2 * tokens * panels * panel,
        ),
        name="ffn",
    )(x, mixed, cot, wo, small, bias, w_in, w_out)


def document_of(positions, lengths, seq_len):
    count = lengths.shape[1]
    order = jnp.arange(count)
    ends = jnp.sum(jnp.where(order[None, :] <= order[:, None], lengths[:, None, :], 0), axis=2)
    counted = jnp.sum((positions[None, :, None] >= ends[:, None, :]).astype(jnp.int32), axis=2)
    inside = (positions >= 0) & (positions < seq_len)
    return jnp.where(inside[None, :], counted, -1)


def masks(lengths, offset, group, seq_len):
    ext = group + 2 * HALO
    slots = ext // 4
    positions = offset - HALO + jnp.arange(ext + PAD, dtype=jnp.int32)
    doc = document_of(positions, lengths, seq_len)
    slot_doc = doc[:, 2:ext:4]
    biases = []
    for block in range(group // QB):
        near = HALO - WIN // 2 + block * QB
        far = block * QB // 4
        key_place = jnp.concatenate((jnp.arange(near, near + NEAR), 4 * jnp.arange(far, far + FAR) + 2))
        reach = jnp.concatenate((jnp.full((NEAR,), WIN // 2), jnp.full((FAR,), PWIN // 2)))
        key_doc = jnp.concatenate((doc[:, near : near + NEAR], slot_doc[:, far : far + FAR]), axis=1)
        query_place = HALO + block * QB + jnp.arange(QB)
        query_doc = doc[:, HALO + block * QB : HALO + (block + 1) * QB]
        allowed = (jnp.abs(key_place[:, None] - query_place[None, :]) <= reach[:, None])[None] & (
            key_doc[:, :, None] == query_doc[:, None, :]
        )
        biases.append(jnp.where(allowed, 0.0, MASKED).astype(F32))
    same = jnp.stack(
        [(doc[:, tap : tap + ext : 4] == slot_doc).astype(F32) for tap in range(5)], axis=1
    )
    same = jnp.broadcast_to(same[..., None], same.shape + (LANES,))
    return jnp.stack(biases, axis=1), same, slots


def local(
    tokens,
    doc_lengths,
    query_weight,
    key_weight,
    value_weight,
    out_weight,
    pool_weight,
    first_gain,
    first_shift,
    inner_weight,
    inner_bias,
    outer_weight,
    outer_bias,
    second_gain,
    second_shift,
    cotangent,
):
    axes = ("dp", "seq")
    seq_count = lax.axis_size("seq")
    parts = lax.axis_size("dp") * seq_count
    seq_place = lax.axis_index("seq")
    seqs, group, width = tokens.shape
    ff = inner_weight.shape[1]
    panels = ff // width
    share = query_weight.shape[0]
    count = seqs * group
    ext = group + 2 * HALO + PAD

    def shift(value, by):
        pairs = [(i, i + by) for i in range(seq_count) if 0 <= i + by < seq_count]
        return lax.ppermute(value, "seq", pairs)

    vectors = jnp.concatenate(
        (
            pool_weight.reshape(-1),
            first_gain,
            first_shift,
            inner_bias,
            outer_bias,
            second_gain,
            second_shift,
        )
    )
    small_rows = -(-vectors.shape[0] // width)
    small_rows += -(3 * share + small_rows) % 8
    vectors_row = jnp.pad(vectors, (0, small_rows * width - vectors.shape[0])).reshape(small_rows, width)
    early = jnp.concatenate((query_weight, key_weight, value_weight, vectors_row), axis=0)
    late = jnp.concatenate(
        (
            out_weight,
            inner_weight.reshape(share, panels, width).transpose(1, 0, 2).reshape(-1, width),
            outer_weight,
        ),
        axis=0,
    )
    early = lax.all_gather(early, axes, axis=0)
    late = lax.all_gather(late, axes, axis=0)
    w_query, w_key, w_value = (
        early[:, i * share : (i + 1) * share].reshape(width, width) for i in range(3)
    )
    small = early[:, 3 * share :].reshape(parts, -1)
    w_out = late[:, :share].reshape(width, width)
    w_inner = (
        late[:, share : (1 + panels) * share]
        .reshape(parts, panels, share, width)
        .transpose(1, 0, 2, 3)
        .reshape(panels, width, width)
    )
    w_outer = late[:, (1 + panels) * share :].reshape(panels, width, width)
    taps = small[:, : 10 * share].reshape(parts, 10, share).transpose(1, 0, 2).reshape(10, width)
    taps = jnp.pad(taps.astype(F32), ((0, 6), (0, 0)))
    at = 10 * share
    vector_list = []
    for size in (share, share, ff // parts, share, share, share):
        vector_list.append(small[:, at : at + size].reshape(1, -1).astype(F32))
        at += size
    gain_one, shift_one, bias_inner, bias_outer, gain_two, shift_two = vector_list
    small_rows_f32 = jnp.concatenate(
        (gain_one, shift_one, bias_outer, gain_two, shift_two, jnp.zeros((3, width), F32)), axis=0
    )
    bias_inner = bias_inner.reshape(panels, 1, width)

    from_left = shift(tokens[:, group - HALO :], 1)
    from_right = shift(tokens[:, :HALO], -1)
    beyond = shift(tokens[:, :1], -2)
    x_ext = jnp.concatenate(
        (from_left, tokens, from_right, jnp.pad(beyond, ((0, 0), (0, PAD - 1), (0, 0)))), axis=1
    )
    flat = tokens.reshape(count, width)
    flat_ext = x_ext.reshape(seqs * ext, width)
    bias, same, slots = masks(doc_lengths, seq_place * group, group, group * seq_count)

    queries = nn(flat, w_query).astype(BF16).reshape(seqs, group, width)
    keys = nn(flat_ext, w_key).astype(BF16).reshape(seqs, ext, width)
    values = nn(flat_ext, w_value).astype(BF16).reshape(seqs, ext, width)
    mixed, lse = attention_forward(queries, keys, values, taps, same, bias)
    y, d_first, d_mixed, d_wo, d_small, d_bias, d_in, d_out = feed_forward(
        flat,
        mixed.reshape(count, width),
        cotangent.reshape(count, width),
        w_out,
        small_rows_f32,
        bias_inner,
        w_inner,
        w_outer,
    )
    late_grads = jnp.concatenate(
        (
            d_wo.reshape(parts, share, width),
            d_in.reshape(panels, parts, share, width)
            .transpose(1, 0, 2, 3)
            .reshape(parts, panels * share, width),
            d_out.reshape(parts, panels * share, width),
        ),
        axis=1,
    )
    late_sum = lax.psum_scatter(
        late_grads.reshape(-1, width), axes, scatter_dimension=0, tiled=True
    ).astype(F32)

    d_queries, d_keys, d_values, d_taps = attention_backward(
        queries, keys, values, taps, same, bias, lse, d_mixed.reshape(seqs, group, width)
    )
    d_queries = d_queries.reshape(count, width)
    d_keys = d_keys.reshape(seqs * ext, width)
    d_values = d_values.reshape(seqs * ext, width)
    d_ext = (nt(d_keys, w_key) + nt(d_values, w_value)).reshape(seqs, ext, width)
    right = HALO + group
    to_left = shift(d_ext[:, :HALO].astype(BF16), -1).astype(F32)
    to_right = shift(d_ext[:, right : right + HALO].astype(BF16), 1).astype(F32)
    to_beyond = shift(d_ext[:, right + HALO : right + HALO + 1].astype(BF16), 2).astype(F32)
    d_query_weight = tn(flat, d_queries).astype(BF16)
    d_key_weight = tn(flat_ext, d_keys).astype(BF16)
    d_value_weight = tn(flat_ext, d_values).astype(BF16)
    d_own = nt(d_queries, w_query) + d_first
    d_input = d_own.reshape(seqs, group, width) + d_ext[:, HALO:right]
    d_input = d_input + jnp.pad(to_left, ((0, 0), (group - HALO, 0), (0, 0)))
    d_input = d_input + jnp.pad(to_right, ((0, 0), (0, group - HALO), (0, 0)))
    d_input = d_input + jnp.pad(to_beyond, ((0, 0), (0, group - 1), (0, 0)))

    d_taps = jnp.sum(d_taps, axis=0)[:10]
    d_vectors = jnp.concatenate(
        [d_taps.reshape(10, parts, share).transpose(1, 0, 2).reshape(parts, 10 * share)]
        + [
            piece.reshape(parts, -1)
            for piece in (d_small[0], d_small[1], d_bias, d_small[2], d_small[3], d_small[4])
        ],
        axis=1,
    )
    d_vectors = jnp.pad(d_vectors, ((0, 0), (0, small_rows * width - d_vectors.shape[1])))
    early_grads = jnp.concatenate(
        [g.reshape(parts, share, width) for g in (d_query_weight, d_key_weight, d_value_weight)]
        + [d_vectors.astype(BF16).reshape(parts, small_rows, width)],
        axis=1,
    )
    early_sum = lax.psum_scatter(
        early_grads.reshape(-1, width), axes, scatter_dimension=0, tiled=True
    ).astype(F32)

    vector_sum = early_sum[3 * share :].reshape(-1)
    pieces = []
    at = 10 * share
    for size in (share, share, ff // parts, share, share, share):
        pieces.append(vector_sum[at : at + size])
        at += size
    return (
        y.reshape(seqs, group, width),
        d_input.astype(BF16),
        early_sum[:share],
        early_sum[share : 2 * share],
        early_sum[2 * share : 3 * share],
        late_sum[:share],
        vector_sum[: 10 * share].reshape(10, share),
        pieces[0],
        pieces[1],
        late_sum[share : (1 + panels) * share]
        .reshape(panels, share, width)
        .transpose(1, 0, 2)
        .reshape(share, ff),
        pieces[2],
        late_sum[(1 + panels) * share :],
        pieces[3],
        pieces[4],
        pieces[5],
    )


def solution(mesh):
    rows = P(("dp", "seq"), None)
    vector = P(("dp", "seq"))
    whole = P("dp", "seq", None)
    taps = P(None, ("dp", "seq"))
    weights = (rows, rows, rows, rows, taps, vector, vector, rows, vector, rows, vector, vector, vector)
    return jax.shard_map(
        local,
        mesh=mesh,
        in_specs=(whole, P("dp", None)) + weights + (whole,),
        out_specs=(whole, whole) + weights,
        check_vma=False,
    )
```

time: 1230 us -> 578 us (0.47)
  waiting for transfers between devices: 502 us -> 284 us
  matrix products: 241 us -> 49.8 us
  blocking collectives: 148 us -> 0 us
  Pallas kernels: 0 us -> 125 us
  local copies, waits for them, and re-layouts: 150 us -> 57.5 us
  other arithmetic: 111 us -> 24 us
  starting transfers between devices: 49.9 us -> 16.4 us
    dot_general x60 -> x9, matrix products: 241 us -> 49.8 us  [the longest x3 17.3 us: nt(): lax.dot_general(left, right, (((1,), (1,)), ((), ())), preferred_element_...]
    unnamed x15 -> x4, waiting for transfers between devices: 186 us -> 0.07 us
    pallas_call x0 -> x3, Pallas kernels: none -> 125 us  [the longest x1 60.5 us: feed_forward(): pl.pallas_call(functools.partial(ffn_kernel, panels), grid=(2 * panels,),...]
    reduce_scatter x3 -> x2, waiting for transfers between devices: 283 us -> 168 us  [the longest x1 143 us: local(): lax.psum_scatter(late_grads.reshape(-1, width), axes, scatter_dimension=0...]
    unnamed x2 -> x0, blocking collectives: 82.3 us -> none
    ppermute x16 -> x6, waiting for transfers between devices: 6.93 us -> 86.5 us  [shift(): return lax.ppermute(value, 'seq', pairs)]
    all_gather x1 -> x0, blocking collectives: 65.7 us -> none  [local(): lax.all_gather(shards[4], ('dp', 'seq'), axis=1, tiled=True)]
    reduce_sum x17 -> x2, other arithmetic: 42.9 us -> 1.77 us  [the longest x1 0.94 us: local(): d_taps = jnp.sum(d_taps, axis=0)[:10]]
  transfers between devices with their start and end apart: 28 -> 10, of which waited for: 8 -> 7; matrix products, arithmetic and copies ran while one was open for 30% -> 13% of each run, Pallas kernels for 0% -> 5%
where the time goes in v1:
time: 578 us; the launch traced here: 571 us
  waiting for transfers between devices  284 us (49%)
  Pallas kernels  125 us (22%)
  local copies, waits for them, and re-layouts  57.5 us (10%)
  matrix products  49.8 us (9%)
  other arithmetic  24 us (4%)
  starting transfers between devices  16.4 us (3%)
  between operations  14.8 us (3%)
    reduce_scatter x1, waiting for transfers between devices, local(): lax.psum_scatter(late_grads.reshape(-1, width), axes, scatter_dimension=0...  143 us
    ppermute x6, waiting for transfers between devices, shift(): return lax.ppermute(value, 'seq', pairs)  86.5 us
    pallas_call x1, Pallas kernels, feed_forward(): pl.pallas_call(functools.partial(ffn_kernel, panels), grid=(2 * panels,),...  60.5 us
    pallas_call x1, Pallas kernels, attention_backward(): pl.pallas_call(attn_bwd_kernel, grid=(seqs, pairs), in_specs=attention_sp...  33.8 us
    pallas_call x1, Pallas kernels, attention_forward(): pl.pallas_call(attn_fwd_kernel, grid=(seqs, pairs), in_specs=attention_sp...  30.4 us
    all_gather x1, waiting for transfers between devices, local(): late = lax.all_gather(late, axes, axis=0)  29.5 us
    reduce_scatter x1, waiting for transfers between devices, local(): lax.psum_scatter(early_grads.reshape(-1, width), axes, scatter_dimension=...  25.3 us
    dot_general x3, matrix products, nt(): lax.dot_general(left, right, (((1,), (1,)), ((), ())), preferred_element_...  17.3 us
  transfers between devices with their start and end apart: 10, of which 7 were waited for; matrix products, arithmetic and copies ran while one was open for 13% of the time, Pallas kernels for 5%

profile of v1, /device:TPU:16, one launch (start us, length us, event | category | flops | bytes accessed | tf_op | source)
XLA Modules:
  0.0 571.5 jit_solution(10938654943727268805)
XLA Ops:
  7.2 0.9 reshape.385
  8.1 4.1 concatenate.37
  12.3 1.5 pad_maximum_fusion.4
  13.8 0.9 copy.112
  14.7 1.7 pad_maximum_fusion.3
  16.5 2.4 collective-permute-start.1
  18.8 3.6 collective-permute-start
  22.4 0.8 slice.166
  23.3 2.8 collective-permute-start.2
  26.2 0.8 select_reduce_fusion
  28.8 0.9 abs_compare_fusion.1
  30.2 1.3 pad_maximum_fusion.2.bias_ref
  32.2 28.9 %collective-permute-done.2 = bf16[4,1,768]{2,1,0:T(2,128)(2,1)S(1)} collective-permute-done((bf16[4,1,768]{2,1,0:T(2,128)(2,1)S(1)}, bf16[4,1,768]{2,1,0:T(2,128)(2,1)S(1)}, u32[]{:S(2)}, u32[]{:S(2)}) %collective-permute-start.2) | collective-permute-done | bytes 6176 | tf_op jit(solution)/shard_map/ppermute | solution.py:532
  61.0 1.8 collective-permute-done.1
  62.8 10.8 %collective-permute-done = bf16[4,256,768]{2,1,0:T(8,128)(2,1)} collective-permute-done((bf16[4,256,768]{2,1,0:T(8,128)(2,1)}, bf16[4,256,768]{2,1,0:T(8,128)(2,1)}, u32[]{:S(2)}, u32[]{:S(2)}) %collective-permute-start) | collective-permute-done | bytes 1572896 | tf_op jit(solution)/shard_map/ppermute | solution.py:532
  73.6 4.6 fusion.1
  78.3 1.0 slice.220
  79.4 0.7 reshape.431.bias_ref
  81.1 3.7 fusion.11
  84.8 1.0 copy-done.16
  85.8 1.4 fusion.6
  87.2 0.7 copy.95
  88.6 7.0 %convolution_convert_fusion = bf16[3136,768]{1,0:T(8,128)(2,1)S(1)} fusion(bf16[3136,768]{1,0:T(8,128)(2,1)} %bitcast.118, bf16[768,768]{1,0:T(8,128)(2,1)} %bitcast.135), kind=kOutput, calls=%fused_computation.4 | convolution fusion | flops 3701784576 | bytes 10813440 | tf_op jit(solution)/shard_map/dot_general | solution.py:38
  95.6 8.5 %convolution_convert_fusion.1 = bf16[3136,768]{1,0:T(8,128)(2,1)S(1)} fusion(bf16[3136,768]{1,0:T(8,128)(2,1)} %bitcast.119, bf16[768,768]{1,0:T(8,128)(2,1)S(1)} %bitcast.137), kind=kOutput, calls=%fused_computation.5 | convolution fusion | flops 3701784576 | bytes 10813440 | tf_op jit(solution)/shard_map/dot_general | solution.py:38
  104.7 30.4 %attn_fwd.1 = (bf16[4,256,768]{2,1,0:T(8,128)(2,1)S(1)}, f32[4,6,2,256]{3,2,1,0:T(2,128)S(1)}) custom-call(bf16[4,256,768]{2,1,0:T(8,128)(2,1)S(1)} %bitcast.94, bf16[4,784,768]{2,1,0:T(8,128)(2,1)S(1)} %bitcast.105, bf16[4,784,768]{2,1,0:T(8,128)(2,1)S(1)} %bitcast.103, f32[16,768]{1,0:T(8,128)S(1)} %pad_convert_fusion.w_ref, ...), custom_call_target="tpu_custom_call" | custom-call | flops 5234491392 | bytes 12779520 | tf_op jit(solution)/shard_map/attn_fwd/pallas_call | solution.py:186
  135.2 2.1 copy-done.11
  137.3 1.1 copy-done.13
  139.0 29.5 %all-gather.7.cloned.1.call-done = bf16[6912,768]{1,0:T(8,128)(2,1)} async-done(((bf16[216,768]{1,0:T(8,128)(2,1)}), bf16[6912,768]{1,0:T(8,128)(2,1)}) %all-gather.7.cloned.1.call-update) | async-done | bytes 10616848 | tf_op jit(solution)/shard_map/all_gather | solution.py:558
  168.5 2.4 slice.228
  170.9 6.6 %fusion.9 = (bf16[32,96,768]{2,1,0:T(8,128)(2,1)}, bf16[32,96,768]{2,1,0:T(8,128)(2,1)S(1)}) fusion(bf16[32,216,768]{2,1,0:T(8,128)(2,1)} %bitcast.117), kind=kLoop, calls=%fused_computation.62 | loop fusion | bytes 18874368 | tf_op jit(solution)/shard_map/slice | solution.py:570
  177.5 2.5 copy.100
  180.0 60.5 %ffn.1 = (bf16[1024,768]{1,0:T(8,128)(2,1)}, f32[1024,768]{1,0:T(8,128)}, bf16[1024,768]{1,0:T(8,128)(2,1)}, bf16[768,768]{1,0:T(8,128)(2,1)}, f32[8,768]{1,0:T(...) custom-call(bf16[1024,768]{1,0:T(8,128)(2,1)} %bitcast.130, ...), custom_call_target="tpu_custom_call" | custom-call | flops 32614907904 | bytes 31457280 | tf_op jit(solution)/shard_map/ffn/pallas_call | solution.py:413
  240.6 1.4 copy-done.1
  242.0 1.4 copy-done.12
  243.4 33.8 %attn_bwd.1 = (bf16[4,256,768]{2,1,0:T(8,128)(2,1)S(1)}, bf16[4,784,768]{2,1,0:T(8,128)(2,1)S(1)}, bf16[4,784,768]{2,1,0:T(8,128)(2,1)S(1)}, f32[4,16,768]{2,1,0:T(8,128)S(1)}) custom-call(bf16[4,256,768]{2,1,0:T(8,128)(2,1)S(1)} %bitcast.95, bf16[4,784,768]{2,1,0:T(8,128)(2,1)} %bitcast.106, bf16[4,784,768]{2,1,0:T(8,128)(2,1)} %bitcast.104, ...), custom_call_target="tpu_custom_call" | custom-call | flops 13086228480 | bytes 23986176 | tf_op jit(solution)/shard_map/attn_bwd/pallas_call | solution.py:220
  277.3 1.1 copy-done.2
  278.4 0.7 copy-done.4
  279.1 2.2 copy-done.7
  281.3 2.3 copy-done.8
  283.6 0.9 reduce_sum.29
  284.5 0.7 convert_reduce_fusion.1
  285.3 0.7 convert.56
  287.2 3.5 bitcast_convert_fusion.2
  290.9 6.4 %bitcast_convert_fusion.1 = bf16[768,768]{1,0:T(8,128)(2,1)S(1)} fusion(bf16[4,784,768]{2,1,0:T(8,128)(2,1)S(1)} %copy-done.9, bf16[4,1,768]{2,1,0:T(2,128)(2,1)S(1)} %collective-permute-done.2, bf16[4,256,768]{2,1,0:T(8,128)(2,1)} %copy-done.21, bf16[4,256,768]{2,1,0:T(8,128)(2,1)S(1)} %copy-done.20, bf16[4,256,768]{2,1,0:T(8,128)(2,1)} %collective-permute-done), kind=kOutput, calls=%fused_computation.14 | convolution fusion | flops 3724050432 | bytes 10721280 | tf_op jit(solution)/shard_map/dot_general | solution.py:34
  297.4 5.8 %bitcast_convert_fusion = bf16[768,768]{1,0:T(8,128)(2,1)S(1)} fusion(bf16[4,784,768]{2,1,0:T(8,128)(2,1)S(1)} %bitcast.98, bf16[4,1,768]{2,1,0:T(2,128)(2,1)S(1)} %collective-permute-done.2, bf16[4,256,768]{2,1,0:T(8,128)(2,1)S(1)} %copy-done.22, bf16[4,256,768]{2,1,0:T(8,128)(2,1)S(1)} %copy-done.20, bf16[4,256,768]{2,1,0:T(8,128)(2,1)} %collective-permute-done), kind=kOutput, calls=%fused_computation.13 | convolution fusion | flops 3724050432 | bytes 10721280 | tf_op jit(solution)/shard_map/dot_general | solution.py:34
  303.1 2.0 pad_maximum_fusion.1
  305.2 3.1 copy.104
  309.3 5.4 pad_maximum_fusion
  314.7 1.3 copy-done.25
  316.0 9.1 %fusion.18 = f32[3136,768]{1,0:T(8,128)} fusion(bf16[3136,768]{1,0:T(8,128)(2,1)} %bitcast.102, bf16[768,768]{1,0:T(8,128)(2,1)S(1)} %bitcast.138), kind=kOutput, calls=%fused_computation.71 | convolution fusion | flops 3699376128 | bytes 15630336 | tf_op jit(solution)/shard_map/dot_general | solution.py:30
  325.1 6.8 %convolution_add_fusion = f32[3136,768]{1,0:T(8,128)S(1)} fusion(f32[3136,768]{1,0:T(8,128)} %fusion.18, bf16[3136,768]{1,0:T(8,128)(2,1)S(1)} %bitcast.101, bf16[768,768]{1,0:T(8,128)(2,1)S(1)} %bitcast.136), kind=kOutput, calls=%fused_computation.3 | convolution fusion | flops 3701784576 | bytes 25264128 | tf_op jit(solution)/shard_map/dot_general | solution.py:30
  332.6 3.1 collective-permute-start.3
  335.7 3.1 collective-permute-start.4
  338.9 1.3 collective-permute-start.5
  340.2 1.4 convolution_add_fusion.1
  341.6 45.0 %collective-permute-done.5 = bf16[4,1,768]{2,1,0:T(2,128)(2,1)S(1)} collective-permute-done((bf16[4,1,768]{2,1,0:T(2,128)(2,1)S(1)}, bf16[4,1,768]{2,1,0:T(2,128)(2,1)S(1)}, u32[]{:S(2)}, u32[]{:S(2)}) %collective-permute-start.5) | collective-permute-done | bytes 6176 | tf_op jit(solution)/shard_map/ppermute | solution.py:532
  386.7 2.0 fusion.5
  388.7 25.3 %reduce-scatter.3.cloned.1.call-done = bf16[80,768]{1,0:T(8,128)(2,1)} async-done(((bf16[2560,768]{1,0:T(8,128)(2,1)}), bf16[80,768]{1,0:T(8,128)(2,1)}) %reduce-scatter.3.cloned.1.call-update) | async-done | bytes 122896 | tf_op jit(solution)/shard_map/reduce_scatter | solution.py:657
  414.0 0.7 slice.251
  416.6 1.5 fusion.13
  418.1 142.7 %reduce-scatter.5.cloned.1.call-done = bf16[216,768]{1,0:T(8,128)(2,1)} async-done(((bf16[6912,768]{1,0:T(8,128)(2,1)}), bf16[216,768]{1,0:T(8,128)(2,1)}) %reduce-scatter.5.cloned.1.call-update) | async-done | bytes 331792 | tf_op jit(solution)/shard_map/reduce_scatter | solution.py:618
  560.8 1.7 fusion.12
  562.5 0.7 copy.108
  563.3 1.4 slice.250
  (143 shorter events, 11.0 us)
Async XLA Ops:
  7.2 66.5 %copy-start.19 = (bf16[4,256,768]{2,1,0:T(8,128)(2,1)S(1)}, bf16[4,256,768]{2,1,0:T(8,128)(2,1)}, u32[]{:S(2)}) copy-start(bf16[4,256,768]{2,1,0:T(8,128)(2,1)} %param.16) | copy-start | bytes 4718596
  7.2 71.1 %all-gather.5.cloned.1.call-start = ((), (), s32[]{:S(2)}) async-start(), calls=%async_computation.4 | async-start | bytes 4055040 | tf_op jit(solution)/shard_map/all_gather | solution.py:557
  13.8 154.8 %all-gather.7.cloned.1.call-start = ((), (), s32[]{:S(2)}) async-start(), calls=%async_computation.5 | async-start | bytes 10948608 | tf_op jit(solution)/shard_map/all_gather | solution.py:558
  16.4 397.5 %reduce-scatter.3.cloned.1.call-start = ((), (), s32[]{:S(2)}) async-start(), calls=%async_computation.2 | async-start | bytes 4055040 | tf_op jit(solution)/shard_map/reduce_scatter | solution.py:657
  16.5 46.3 %collective-permute-start.1 = (bf16[4,256,768]{2,1,0:T(8,128)(2,1)}, bf16[4,256,768]{2,1,0:T(8,128)(2,1)S(1)}, u32[]{:S(2)}, u32[]{:S(2)}) collective-permute-start(bf16[4,256,768]{2,1,0:T(8,128)(2,1)} %param.16), channel_id=1, source_target_pairs={{1,0},{2,1},{3,2},{5,4},{6,5},{7,6},{9,8},{10,9},{11,10},{13,12},{... | collective-permute-start | bytes 4718600 | tf_op jit(solution)/shard_map/ppermute | solution.py:532
  18.8 54.8 %collective-permute-start = (bf16[4,256,768]{2,1,0:T(8,128)(2,1)}, bf16[4,256,768]{2,1,0:T(8,128)(2,1)}, u32[]{:S(2)}, u32[]{:S(2)}) collective-permute-start(bf16[4,256,768]{2,1,0:T(8,128)(2,1)} %param.16), channel_id=1, source_target_pairs={{0,1},{1,2},{2,3},{4,5},{5,6},{6,7},{8,9},{9,10},{10,11},{12,13},{... | collective-permute-start | bytes 4718600 | tf_op jit(solution)/shard_map/ppermute | solution.py:532
  23.3 37.8 %collective-permute-start.2 = (bf16[4,1,768]{2,1,0:T(2,128)(2,1)S(1)}, bf16[4,1,768]{2,1,0:T(2,128)(2,1)S(1)}, u32[]{:S(2)}, u32[]{:S(2)}) collective-permute-start(bf16[4,1,768]{2,1,0:T(2,128)(2,1)S(1)} %slice.166), channel_id=1, source_target_pairs={{2,0},{3,1},{6,4},{7,5},{10,8},{11,9},{14,12},{15,13},{18,16},{19,... | collective-permute-start | bytes 18440 | tf_op jit(solution)/shard_map/ppermute | solution.py:532
  62.8 15.5 %copy-start.21 = (bf16[4,256,768]{2,1,0:T(8,128)(2,1)}, bf16[4,256,768]{2,1,0:T(8,128)(2,1)S(1)}, u32[]{:S(2)}) copy-start(bf16[4,256,768]{2,1,0:T(8,128)(2,1)S(1)} %collective-permute-done.1) | copy-start | bytes 4718596
  84.8 1.0 copy-start.16
  88.6 16.1 %copy-start.5 = (f32[16,768]{1,0:T(8,128)}, f32[16,768]{1,0:T(8,128)S(1)}, u32[]{:S(2)}) copy-start(f32[16,768]{1,0:T(8,128)S(1)} %pad_convert_fusion.w_ref) | copy-start | bytes 147460
  88.6 7.0 %copy-start.24 = (bf16[32,24,768]{2,1,0:T(8,128)(2,1)S(1)}, bf16[32,24,768]{2,1,0:T(8,128)(2,1)}, u32[]{:S(2)}) copy-start(bf16[32,24,768]{2,1,0:T(8,128)(2,1)} %get-tuple-element.53) | copy-start | bytes 3538948
  95.6 9.1 %copy-start.10 = (bf16[3136,768]{1,0:T(8,128)(2,1)}, bf16[3136,768]{1,0:T(8,128)(2,1)S(1)}, u32[]{:S(2)}) copy-start(bf16[3136,768]{1,0:T(8,128)(2,1)S(1)} %convolution_convert_fusion) | copy-start | bytes 14450692
  95.6 8.5 %copy-start.27 = (f32[4,5,192]{2,1,0:T(8,128)S(1)}, f32[4,5,192]{2,1,0:T(8,128)}, u32[]{:S(2)}) copy-start(f32[4,5,192]{2,1,0:T(8,128)} %copy.98) | copy-start | bytes 46084
  95.6 9.1 %copy-start = (f32[4,2,416,128]{3,2,1,0:T(8,128)S(1)}, f32[4,2,416,128]{3,2,1,0:T(8,128)}, u32[]{:S(2)}) copy-start(f32[4,2,416,128]{3,2,1,0:T(8,128)} %pad_maximum_fusion.2.bias_ref) | copy-start | bytes 5111812
  135.1 2.1 copy-start.11
  137.3 1.1 copy-start.13
  138.4 0.6 copy-start.14
  180.0 60.6 %copy-start.6 = (f32[16,768]{1,0:T(8,128)S(1)}, f32[16,768]{1,0:T(8,128)}, u32[]{:S(2)}) copy-start(f32[16,768]{1,0:T(8,128)} %copy-done.5) | copy-start | bytes 147460
  180.0 60.6 %copy-start.15 = (f32[4,6,2,256]{3,2,1,0:T(2,128)S(1)}, f32[4,6,2,256]{3,2,1,0:T(2,128)}, u32[]{:S(2)}) copy-start(f32[4,6,2,256]{3,2,1,0:T(2,128)} %copy-done.14) | copy-start | bytes 147460
  240.6 1.5 copy-start.1
  242.0 1.4 copy-start.12
  277.3 1.1 copy-start.2
  278.4 0.7 copy-start.4
  279.1 2.2 copy-start.7
  281.3 2.3 copy-start.8
  287.1 3.6 copy-start.20
  287.2 3.7 copy-start.9
  287.2 10.1 %slice-start = ((s8[4816896]{0:T(1024)(128)(4,1)}), s8[4194304]{0:T(1024)(128)(4,1)S(1)}, s32[]{:S(2)}) async-start(s8[4816896]{0:T(1024)(128)(4,1)} %bitcast.97), calls=%async_computation.6 | async-start | bytes 8388608
  290.9 6.4 %slice-start.1 = ((s8[4816896]{0:T(1024)(128)(4,1)}), s8[622592]{0:T(1024)(128)(4,1)S(1)}, s32[]{:S(2)}) async-start(s8[4816896]{0:T(1024)(128)(4,1)} %bitcast.97), calls=%async_computation.7 | async-start | bytes 1245184
  290.9 6.4 %copy-start.22 = (bf16[4,256,768]{2,1,0:T(8,128)(2,1)S(1)}, bf16[4,256,768]{2,1,0:T(8,128)(2,1)}, u32[]{:S(2)}) copy-start(bf16[4,256,768]{2,1,0:T(8,128)(2,1)} %copy-done.21) | copy-start | bytes 4718596
  305.1 3.2 slice-start.4
  305.2 255.6 %reduce-scatter.5.cloned.1.call-start = ((), (), s32[]{:S(2)}) async-start(), calls=%async_computation.3 | async-start | bytes 10948608 | tf_op jit(solution)/shard_map/reduce_scatter | solution.py:618
  305.2 3.7 slice-start.5
  305.2 4.1 copy-start.26
  314.6 1.3 copy-start.25
  314.6 10.4 %slice-start.2 = ((s8[4816896]{0:T(1024)(128)(4,1)}), s8[622592]{0:T(1024)(128)(4,1)S(1)}, s32[]{:S(2)}) async-start(s8[4816896]{0:T(1024)(128)(4,1)} %bitcast.99), calls=%async_computation.8 | async-start | bytes 1245184
  315.9 9.1 %slice-start.3 = ((s8[4816896]{0:T(1024)(128)(4,1)}), s8[4194304]{0:T(1024)(128)(4,1)S(1)}, s32[]{:S(2)}) async-start(s8[4816896]{0:T(1024)(128)(4,1)} %bitcast.99), calls=%async_computation.9 | async-start | bytes 8388608
  315.9 9.1 %copy-start.23 = (bf16[32,24,768]{2,1,0:T(8,128)(2,1)S(1)}, bf16[32,24,768]{2,1,0:T(8,128)(2,1)}, u32[]{:S(2)}) copy-start(bf16[32,24,768]{2,1,0:T(8,128)(2,1)} %get-tuple-element.52) | copy-start | bytes 3538948
  332.4 7.8 %copy-start.3 = (bf16[4,256,768]{2,1,0:T(8,128)(2,1)S(1)}, bf16[4,256,768]{2,1,0:T(8,128)(2,1)}, u32[]{:S(2)}) copy-start(bf16[4,256,768]{2,1,0:T(8,128)(2,1)} %copy-done.2) | copy-start | bytes 4718596
  332.4 7.8 %copy-start.17 = (bf16[32,24,768]{2,1,0:T(8,128)(2,1)S(1)}, bf16[32,24,768]{2,1,0:T(8,128)(2,1)}, u32[]{:S(2)}) copy-start(bf16[32,24,768]{2,1,0:T(8,128)(2,1)} %copy-done.16) | copy-start | bytes 3538948
  332.4 7.8 %copy-start.18 = (f32[1024,768]{1,0:T(8,128)S(1)}, f32[1024,768]{1,0:T(8,128)}, u32[]{:S(2)}) copy-start(f32[1024,768]{1,0:T(8,128)} %get-tuple-element.34) | copy-start | bytes 9437188
  332.6 54.0 %collective-permute-start.3 = (bf16[4,256,768]{2,1,0:T(8,128)(2,1)S(1)}, bf16[4,256,768]{2,1,0:T(8,128)(2,1)S(1)}, u32[]{:S(2)}, u32[]{:S(2)}) collective-permute-start(bf16[4,256,768]{2,1,0:T(8,128)(2,1)S(1)} %get-tuple-element.50), channel_id=1, source_target_pairs={{1,0},{2,1},{3,2},{5,4},{6,5},{7,6},{9,8},{10,9},{11,10},{13,12},{... | collective-permute-start | bytes 4718600 | tf_op jit(solution)/shard_map/ppermute | solution.py:532
  335.7 50.9 %collective-permute-start.4 = (bf16[4,256,768]{2,1,0:T(8,128)(2,1)S(1)}, bf16[4,256,768]{2,1,0:T(8,128)(2,1)S(1)}, u32[]{:S(2)}, u32[]{:S(2)}) collective-permute-start(bf16[4,256,768]{2,1,0:T(8,128)(2,1)S(1)} %get-tuple-element.51), channel_id=1, source_target_pairs={{0,1},{1,2},{2,3},{4,5},{5,6},{6,7},{8,9},{9,10},{10,11},{12,13},{... | collective-permute-start | bytes 4718600 | tf_op jit(solution)/shard_map/ppermute | solution.py:532
  338.9 47.8 %collective-permute-start.5 = (bf16[4,1,768]{2,1,0:T(2,128)(2,1)S(1)}, bf16[4,1,768]{2,1,0:T(2,128)(2,1)S(1)}, u32[]{:S(2)}, u32[]{:S(2)}) collective-permute-start(bf16[4,1,768]{2,1,0:T(2,128)(2,1)S(1)} %slice.240), channel_id=1, source_target_pairs={{0,2},{1,3},{4,6},{5,7},{8,10},{9,11},{12,14},{13,15},{16,18},{17,... | collective-permute-start | bytes 18440 | tf_op jit(solution)/shard_map/ppermute | solution.py:532
Sparse Core Ops, SparseCore 0:
  13.9 63.7 all-gather.4
  81.1 87.4 all-gather.6
  305.3 108.6 reduce-scatter.2
  419.9 140.8 reduce-scatter.4

commit v2 on v1

v2 whole, which is shorter than its diff:
```python
import functools

import jax
import jax.numpy as jnp
from jax import lax
from jax.experimental import pallas as pl
from jax.experimental.pallas import tpu as pltpu
from jax.sharding import Mesh
from jax.sharding import PartitionSpec as P

HEADS = 12
HEAD_DIM = 64
WIN = 128
PWIN = 512
EPS = 1e-05

LANES = 128
QB = 128
GROUP = 6
GROUP_BACK = 2
HALO = PWIN // 2
PAD = 16
NEAR = QB + WIN
FAR = (QB + PWIN) // 4
KEYS = NEAR + FAR
MASKED = -1e30
QUICK = pl.CostEstimate(flops=1 << 20, bytes_accessed=1 << 20, transcendentals=0)

F32 = jnp.float32
BF16 = jnp.bfloat16


def nt(left, right):
    return lax.dot_general(left, right, (((1,), (1,)), ((), ())), preferred_element_type=F32)


def tn(left, right):
    return lax.dot_general(left, right, (((0,), (0,)), ((), ())), preferred_element_type=F32)


def nn(left, right):
    return lax.dot_general(left, right, (((1,), (0,)), ((), ())), preferred_element_type=F32)


def slot_taps(wide, slots):
    return [wide[pl.ds(tap, slots, stride=4), :] for tap in range(5)]


def pool(taps, same_ref, w_ref, first, lanes):
    total = None
    for tap in range(5):
        term = taps[tap] * same_ref[0, tap] * w_ref[first + tap : first + tap + 1, lanes]
        total = term if total is None else total + term
    return total.astype(BF16)


def pair_stack(rows):
    lane = lax.broadcasted_iota(jnp.int32, rows.shape, 1)
    zero = jnp.zeros_like(rows)
    return jnp.concatenate(
        (jnp.where(lane < HEAD_DIM, rows, zero), jnp.where(lane < HEAD_DIM, zero, rows)), axis=0
    )


def pair_join(both):
    joined = jnp.concatenate((both[:HEAD_DIM, :QB], both[HEAD_DIM:, QB:]), axis=0)
    return joined.T


def rows_of(block):
    return slice(block * QB, (block + 1) * QB)


def keys_of(ref, pooled, block, lanes):
    near = HALO - WIN // 2 + block * QB
    far = block * QB // 4
    return jnp.concatenate((ref[0, near : near + NEAR, lanes], pooled[far : far + FAR, :]), axis=0)


def scores_of(keys, stacked, bias):
    return nt(keys, stacked) + jnp.concatenate((bias, bias), axis=1)


def attn_fwd_kernel(
    q_ref, k_ref, v_ref, w_ref, same_ref, bias_ref, out_ref, lse_ref, k_wide, v_wide, pk_ref, pv_ref
):
    slots = pk_ref.shape[1]
    scale = jnp.asarray(HEAD_DIM**-0.5, BF16)

    blocks = q_ref.shape[1] // QB

    def body(step, carry):
        jobs = []
        for lane in range(GROUP):
            pair = step * GROUP + lane
            lanes = pl.ds(pl.multiple_of(pair * LANES, LANES), LANES)
            k_wide[lane] = k_ref[0, :, lanes].astype(F32)
            v_wide[lane] = v_ref[0, :, lanes].astype(F32)
            pk_ref[lane] = pool(slot_taps(k_wide.at[lane], slots), same_ref, w_ref, 0, lanes)
            pv_ref[lane] = pool(slot_taps(v_wide.at[lane], slots), same_ref, w_ref, 5, lanes)
            jobs += [(lane, pair, lanes, block) for block in range(blocks)]
        scores = []
        for lane, pair, lanes, block in jobs:
            stacked = pair_stack(q_ref[0, rows_of(block), lanes] * scale)
            keys = keys_of(k_ref, pk_ref.at[lane], block, lanes)
            scores.append(scores_of(keys, stacked, bias_ref[0, block]))
        probs = []
        for (lane, pair, lanes, block), score in zip(jobs, scores):
            top = jnp.max(score, axis=0, keepdims=True)
            weights = jnp.exp(score - top)
            denom = jnp.sum(weights, axis=0, keepdims=True)
            probs.append((weights * (1.0 / denom)).astype(BF16))
            lse_ref[0, pair, block : block + 1, :] = top + jnp.log(denom)
        mixed = []
        for (lane, pair, lanes, block), prob in zip(jobs, probs):
            mixed.append(tn(keys_of(v_ref, pv_ref.at[lane], block, lanes), prob))
        for (lane, pair, lanes, block), value in zip(jobs, mixed):
            out_ref[0, rows_of(block), lanes] = pair_join(value).astype(BF16)
        return carry

    lax.fori_loop(0, q_ref.shape[2] // (LANES * GROUP), body, 0)


def attn_bwd_kernel(
    q_ref,
    k_ref,
    v_ref,
    w_ref,
    same_ref,
    bias_ref,
    lse_ref,
    do_ref,
    dq_ref,
    dk_ref,
    dv_ref,
    dw_ref,
    k_wide,
    v_wide,
    pk_ref,
    pv_ref,
    dpk_ref,
    dpv_ref,
):
    slots = pk_ref.shape[1]
    scale = jnp.asarray(HEAD_DIM**-0.5, BF16)
    blocks = q_ref.shape[1] // QB

    def body(step, carry):
        jobs = []
        for lane in range(GROUP_BACK):
            pair = step * GROUP_BACK + lane
            lanes = pl.ds(pl.multiple_of(pair * LANES, LANES), LANES)
            k_wide[lane] = k_ref[0, :, lanes].astype(F32)
            v_wide[lane] = v_ref[0, :, lanes].astype(F32)
            pk_ref[lane] = pool(slot_taps(k_wide.at[lane], slots), same_ref, w_ref, 0, lanes)
            pv_ref[lane] = pool(slot_taps(v_wide.at[lane], slots), same_ref, w_ref, 5, lanes)
            jobs += [(lane, pair, lanes, block) for block in range(blocks)]
        dpk_ref[...] = jnp.zeros_like(dpk_ref)
        dpv_ref[...] = jnp.zeros_like(dpv_ref)
        scores, d_probs = [], []
        for lane, pair, lanes, block in jobs:
            keys = keys_of(k_ref, pk_ref.at[lane], block, lanes)
            stacked = pair_stack(q_ref[0, rows_of(block), lanes] * scale)
            scores.append(scores_of(keys, stacked, bias_ref[0, block]))
            values = keys_of(v_ref, pv_ref.at[lane], block, lanes)
            d_probs.append(nt(values, pair_stack(do_ref[0, rows_of(block), lanes])))
        probs, d_scores = [], []
        for (lane, pair, lanes, block), score, d_prob in zip(jobs, scores, d_probs):
            prob = jnp.exp(score - lse_ref[0, pair, block : block + 1, :])
            row_dot = jnp.sum(prob * d_prob, axis=0, keepdims=True)
            d_scores.append((prob * (d_prob - row_dot)).astype(BF16))
            probs.append(prob.astype(BF16))
        parts = []
        for (lane, pair, lanes, block), prob, d_score in zip(jobs, probs, d_scores):
            d_values = nn(prob, pair_stack(do_ref[0, rows_of(block), lanes]))
            d_keys = nn(d_score, pair_stack(q_ref[0, rows_of(block), lanes] * scale))
            far = slice(block * QB // 4, block * QB // 4 + FAR)
            dpk_ref[lane, far, :] += d_keys[NEAR:]
            dpv_ref[lane, far, :] += d_values[NEAR:]
            parts.append((d_keys[:NEAR], d_values[:NEAR]))
        d_queries = []
        for (lane, pair, lanes, block), d_score in zip(jobs, d_scores):
            d_queries.append(tn(keys_of(k_ref, pk_ref.at[lane], block, lanes), d_score))
        for (lane, pair, lanes, block), value in zip(jobs, d_queries):
            dq_ref[0, rows_of(block), lanes] = (pair_join(value) * HEAD_DIM**-0.5).astype(BF16)
        for lane in range(GROUP_BACK):
            lanes = jobs[lane * blocks][2]
            for side, (wide_ref, d_pool_ref, out_ref) in enumerate(
                ((k_wide, dpk_ref, dk_ref), (v_wide, dpv_ref, dv_ref))
            ):
                wide = wide_ref.at[lane]
                d_pool = d_pool_ref[lane]
                taps = slot_taps(wide, slots)
                masked = [d_pool * same_ref[0, tap] for tap in range(5)]
                places = [5 * side + tap for tap in range(5)]
                for tap, row in enumerate(places):
                    dw_ref[0, row : row + 1, lanes] = jnp.sum(
                        masked[tap] * taps[tap], axis=0, keepdims=True
                    )
                spread = [
                    masked[tap] * w_ref[row : row + 1, lanes] for tap, row in enumerate(places)
                ]
                wide[4 * slots :, :] = jnp.zeros((wide.shape[0] - 4 * slots, LANES), F32)
                for tap in range(4):
                    wide[pl.ds(tap, slots, stride=4), :] = spread[tap]
                wide[pl.ds(4, slots, stride=4), :] += spread[4]
                for block in range(blocks):
                    near = HALO - WIN // 2 + block * QB
                    wide[near : near + NEAR, :] += parts[lane * blocks + block][side]
                out_ref[0, :, lanes] = wide[...].astype(BF16)
        return carry

    lax.fori_loop(0, q_ref.shape[2] // (LANES * GROUP_BACK), body, 0)
    dw_ref[0, 10:, :] = jnp.zeros((dw_ref.shape[1] - 10, dw_ref.shape[2]), F32)


def by_seq(*shape, first=0):
    return pl.BlockSpec((1,) + shape, lambda s: (s + first,) + (0,) * len(shape))


def attention_specs(ext, group, slots, width, first=0):
    return [
        by_seq(group, width, first=first),
        by_seq(ext, width, first=first),
        by_seq(ext, width, first=first),
        pl.BlockSpec((16, width), lambda s: (0, 0)),
        by_seq(5, slots, LANES, first=first),
        by_seq(group // QB, KEYS, LANES, first=first),
    ]


def attention_forward(queries, keys, values, taps, same, bias):
    seqs, group, width = queries.shape
    ext = keys.shape[1]
    slots = same.shape[2]
    pairs = width // LANES
    blocks = group // QB
    wide = pltpu.VMEM((GROUP, ext, LANES), F32)
    pooled = pltpu.VMEM((GROUP, slots, LANES), BF16)
    return pl.pallas_call(
        attn_fwd_kernel,
        grid=(seqs,),
        in_specs=attention_specs(ext, group, slots, width),
        out_specs=[by_seq(group, width), by_seq(pairs, blocks, 2 * QB)],
        out_shape=[
            jax.ShapeDtypeStruct((seqs, group, width), BF16),
            jax.ShapeDtypeStruct((seqs, pairs, blocks, 2 * QB), F32),
        ],
        scratch_shapes=[wide, wide, pooled, pooled],
        compiler_params=pltpu.CompilerParams(vmem_limit_bytes=48 << 20),
        cost_estimate=QUICK,
        name="attn_fwd",
    )(queries, keys, values, taps, same, bias)


def attention_backward(queries, keys, values, taps, same, bias, lse, d_mixed, first, count, earlier):
    seqs, group, width = queries.shape
    ext = keys.shape[1]
    slots = same.shape[2]
    pairs = width // LANES
    blocks = group // QB
    wide = pltpu.VMEM((GROUP_BACK, ext, LANES), F32)
    pooled = pltpu.VMEM((GROUP_BACK, slots, LANES), BF16)
    d_pooled = pltpu.VMEM((GROUP_BACK, slots, LANES), F32)
    args = (queries, keys, values, taps, same, bias, lse, d_mixed)

    def kernel(*refs):
        attn_bwd_kernel(*refs[: len(args)], *refs[len(args) + len(earlier) :])

    return pl.pallas_call(
        kernel,
        grid=(count,),
        in_specs=attention_specs(ext, group, slots, width, first)
        + [by_seq(pairs, blocks, 2 * QB, first=first), by_seq(group, width, first=first)]
        + [pl.BlockSpec(memory_space=pl.ANY)] * len(earlier),
        out_specs=[
            by_seq(*shape, first=first)
            for shape in ((group, width), (ext, width), (ext, width), (16, width))
        ],
        out_shape=[
            jax.ShapeDtypeStruct((seqs, group, width), BF16),
            jax.ShapeDtypeStruct((seqs, ext, width), BF16),
            jax.ShapeDtypeStruct((seqs, ext, width), BF16),
            jax.ShapeDtypeStruct((seqs, 16, width), F32),
        ],
        input_output_aliases={len(args) + i: i for i in range(len(earlier))},
        scratch_shapes=[wide, wide, pooled, pooled, d_pooled, d_pooled],
        compiler_params=pltpu.CompilerParams(vmem_limit_bytes=48 << 20),
        cost_estimate=QUICK,
        name="attn_bwd",
    )(*args, *earlier)


ROWS = 1024
HALF_PI = 0.3989422804014327


def row_sum(value):
    return jnp.sum(value, axis=0, keepdims=True)


def row_mean(value):
    return jnp.mean(value, axis=1, keepdims=True)


def normalize(value):
    centered = value - row_mean(value)
    inv = lax.rsqrt(row_mean(centered * centered) + EPS)
    return centered * inv, inv


def normalize_back(grad, normed, inv):
    return inv * (grad - row_mean(grad) - normed * row_mean(grad * normed))


def split_cores(value, core, per_core):
    both = value.reshape(-1, 2, per_core, value.shape[1])
    mine = jnp.where(core == 0, both[:, 0], both[:, 1])
    other = jnp.where(core == 0, both[:, 1], both[:, 0])
    return mine.astype(BF16), other.astype(BF16)


def ffn_kernel(
    panels,
    core_ref,
    x_ref,
    mixed_ref,
    cot_ref,
    wo_ref,
    small_ref,
    bias_ref,
    w_in_ref,
    w_out_ref,
    y_ref,
    d_first_ref,
    d_mixed_ref,
    d_small_ref,
    d_bias_ref,
    d_wo_ref,
    d_wo_other_ref,
    d_in_ref,
    d_in_other_ref,
    d_out_ref,
    d_out_other_ref,
    n_one,
    inv_one,
    low,
    hidden,
    slope,
    d_inner,
):
    step = pl.program_id(0)
    tokens, width = x_ref.shape
    chunks = tokens // ROWS
    acc, d_outer = d_first_ref, d_mixed_ref
    core = core_ref[0]
    rows_in, rows_out = d_in_ref.shape[2], d_out_ref.shape[1]

    def square(ref):
        return ref[...].reshape(width, width)

    gain_one, shift_one, outer_bias, gain_two, shift_two = (
        small_ref[i : i + 1, :] for i in range(5)
    )

    @pl.when(step == 0)
    def _():
        def body(i, carry):
            rows = pl.ds(pl.multiple_of(i * ROWS, ROWS), ROWS)
            first = x_ref[rows, :].astype(F32) + nn(mixed_ref[rows, :], square(wo_ref))
            normed, inv = normalize(first)
            n_one[rows, :] = normed
            inv_one[rows, :] = jnp.broadcast_to(inv, (ROWS, LANES))
            out = normed * gain_one + shift_one
            low[rows, :] = out.astype(BF16)
            acc[rows, :] = out + outer_bias
            return carry

        lax.fori_loop(0, chunks, body, 0)

    @pl.when(step < panels)
    def _():
        def body(i, carry):
            rows = pl.ds(pl.multiple_of(i * ROWS, ROWS), ROWS)
            inner = nn(low[rows, :], square(w_in_ref)) + bias_ref[0]
            cdf = 0.5 * (1.0 + lax.erf(inner * 0.7071067811865476))
            pdf = HALF_PI * jnp.exp(-0.5 * inner * inner)
            out = (inner * cdf).astype(BF16)
            hidden[step, rows, :] = out
            slope[step, rows, :] = cdf + inner * pdf
            acc[rows, :] += nn(out, square(w_out_ref))
            return carry

        lax.fori_loop(0, chunks, body, 0)

    @pl.when(step == panels)
    def _():
        def body(i, carry):
            d_gain, d_shift, d_bias = carry
            rows = pl.ds(pl.multiple_of(i * ROWS, ROWS), ROWS)
            normed, inv = normalize(acc[rows, :])
            y_ref[rows, :] = (normed * gain_two + shift_two).astype(BF16)
            grad = cot_ref[rows, :].astype(F32)
            d_second = normalize_back(grad * gain_two, normed, inv)
            low_grad = d_second.astype(BF16)
            acc[rows, :] = d_second
            d_outer[rows, :] = low_grad
            return (
                d_gain + row_sum(grad * normed),
                d_shift + row_sum(grad),
                d_bias + row_sum(low_grad.astype(F32)),
            )

        zero = jnp.zeros((1, width), F32)
        d_gain, d_shift, d_bias = lax.fori_loop(0, chunks, body, (zero, zero, zero))
        d_small_ref[2:3, :] = d_bias
        d_small_ref[3:4, :] = d_gain
        d_small_ref[4:5, :] = d_shift
        d_small_ref[5:, :] = jnp.zeros((3, width), F32)

    @pl.when(step >= panels)
    def _():
        panel = step - panels

        def body(i, d_bias):
            rows = pl.ds(pl.multiple_of(i * ROWS, ROWS), ROWS)
            d_hidden = nt(d_outer[rows, :], square(w_out_ref))
            grad = (d_hidden * slope[panel, rows, :]).astype(BF16)
            d_inner[rows, :] = grad
            acc[rows, :] += nt(grad, square(w_in_ref))
            return d_bias + row_sum(grad.astype(F32))

        d_bias_ref[0] = lax.fori_loop(0, chunks, body, jnp.zeros(d_bias_ref.shape[1:], F32))
        d_out_ref[...], d_out_other_ref[...] = split_cores(
            tn(hidden[panel], d_outer[...]), core, rows_out
        )
        d_in_ref[:, 0], d_in_other_ref[:, 0] = split_cores(
            tn(low[...], d_inner[...]), core, rows_in
        )

    @pl.when(step == 2 * panels - 1)
    def _():
        def body(i, carry):
            d_gain, d_shift = carry
            rows = pl.ds(pl.multiple_of(i * ROWS, ROWS), ROWS)
            grad = acc[rows, :]
            normed = n_one[rows, :]
            d_first = normalize_back(grad * gain_one, normed, inv_one[rows, 0:1])
            d_first_ref[rows, :] = d_first
            low_grad = d_first.astype(BF16)
            d_inner[rows, :] = low_grad
            d_mixed_ref[rows, :] = nt(low_grad, square(wo_ref)).astype(BF16)
            return d_gain + row_sum(grad * normed), d_shift + row_sum(grad)

        zero = jnp.zeros((1, width), F32)
        d_gain, d_shift = lax.fori_loop(0, chunks, body, (zero, zero))
        d_small_ref[0:1, :] = d_gain
        d_small_ref[1:2, :] = d_shift
        d_wo_ref[...], d_wo_other_ref[...] = split_cores(
            tn(mixed_ref[...], d_inner[...]), core, rows_in
        )


def feed_forward(core, x, mixed, cot, small, bias, weights):
    tokens, width = x.shape
    units, groups, rows_in, _ = weights.shape
    panels = groups // 2
    panel = width
    chips = units // 2
    rows_out = panels * rows_in

    def whole(*shape):
        return pl.BlockSpec(
            shape, lambda j: (0,) * len(shape), pipeline_mode=pl.Buffered(buffer_count=1)
        )

    def later(j):
        return jnp.maximum(j - panels, 0)

    d_in = pl.BlockSpec((chips, 1, rows_in, width), lambda j: (0, later(j), 0, 0))
    d_out = pl.BlockSpec((chips // panels, rows_out, width), lambda j: (later(j), 0, 0))
    return pl.pallas_call(
        functools.partial(ffn_kernel, panels),
        grid=(2 * panels,),
        in_specs=[
            pl.BlockSpec(memory_space=pltpu.SMEM),
            whole(tokens, width),
            whole(tokens, width),
            whole(tokens, width),
            pl.BlockSpec(
                (units, 1, rows_in, width),
                lambda j: (0, 2 * panels, 0, 0),
                pipeline_mode=pl.Buffered(buffer_count=1),
            ),
            whole(8, width),
            pl.BlockSpec((1, 1, panel), lambda j: (lax.rem(j, panels), 0, 0)),
            pl.BlockSpec((units, 1, rows_in, width), lambda j: (0, panels + lax.rem(j, panels), 0, 0)),
            pl.BlockSpec(
                (units // panels, panels, rows_in, width), lambda j: (lax.rem(j, panels), 0, 0, 0)
            ),
        ],
        out_specs=[
            whole(tokens, width),
            whole(tokens, width),
            whole(tokens, width),
            whole(8, width),
            pl.BlockSpec((1, 1, panel), lambda j: (later(j), 0, 0)),
            whole(chips, rows_in, width),
            whole(chips, rows_in, width),
            d_in,
            d_in,
            d_out,
            d_out,
        ],
        out_shape=[
            jax.ShapeDtypeStruct((tokens, width), BF16),
            jax.ShapeDtypeStruct((tokens, width), F32),
            jax.ShapeDtypeStruct((tokens, width), BF16),
            jax.ShapeDtypeStruct((8, width), F32),
            jax.ShapeDtypeStruct((panels, 1, panel), F32),
        ]
        + [jax.ShapeDtypeStruct((chips, rows_in, width), BF16)] * 2
        + [jax.ShapeDtypeStruct((chips, panels, rows_in, width), BF16)] * 2
        + [jax.ShapeDtypeStruct((chips, rows_out, width), BF16)] * 2,
        scratch_shapes=[
            pltpu.VMEM((tokens, width), F32),
            pltpu.VMEM((tokens, LANES), F32),
            pltpu.VMEM((tokens, width), BF16),
            pltpu.VMEM((panels, tokens, panel), BF16),
            pltpu.VMEM((panels, tokens, panel), F32),
            pltpu.VMEM((tokens, panel), BF16),
        ],
        compiler_params=pltpu.CompilerParams(vmem_limit_bytes=60 << 20),
        cost_estimate=QUICK,
        name="ffn",
    )(core, x, mixed, cot, weights, small, bias, weights, weights)


def document_of(positions, lengths, seq_len):
    count = lengths.shape[1]
    order = jnp.arange(count)
    ends = jnp.sum(jnp.where(order[None, :] <= order[:, None], lengths[:, None, :], 0), axis=2)
    counted = jnp.sum((positions[None, :, None] >= ends[:, None, :]).astype(jnp.int32), axis=2)
    inside = (positions >= 0) & (positions < seq_len)
    return jnp.where(inside[None, :], counted, -1)


def masks(lengths, offset, group, seq_len):
    ext = group + 2 * HALO
    slots = ext // 4
    positions = offset - HALO + jnp.arange(ext + PAD, dtype=jnp.int32)
    doc = document_of(positions, lengths, seq_len)
    slot_doc = doc[:, 2:ext:4]
    biases = []
    for block in range(group // QB):
        near = HALO - WIN // 2 + block * QB
        far = block * QB // 4
        key_place = jnp.concatenate((jnp.arange(near, near + NEAR), 4 * jnp.arange(far, far + FAR) + 2))
        reach = jnp.concatenate((jnp.full((NEAR,), WIN // 2), jnp.full((FAR,), PWIN // 2)))
        key_doc = jnp.concatenate((doc[:, near : near + NEAR], slot_doc[:, far : far + FAR]), axis=1)
        query_place = HALO + block * QB + jnp.arange(QB)
        query_doc = doc[:, HALO + block * QB : HALO + (block + 1) * QB]
        allowed = (jnp.abs(key_place[:, None] - query_place[None, :]) <= reach[:, None])[None] & (
            key_doc[:, :, None] == query_doc[:, None, :]
        )
        biases.append(jnp.where(allowed, 0.0, MASKED).astype(F32))
    same = jnp.stack(
        [(doc[:, tap : tap + ext : 4] == slot_doc).astype(F32) for tap in range(5)], axis=1
    )
    same = jnp.broadcast_to(same[..., None], same.shape + (LANES,))
    return jnp.stack(biases, axis=1), same, slots


def steps(count):
    for k in range(1, count):
        if count & (count - 1) == 0:
            yield [(i, i ^ k) for i in range(count)], lambda me, k=k: (me ^ k, me ^ k)
        else:
            yield (
                [(i, (i + k) % count) for i in range(count)],
                lambda me, k=k: (lax.rem(me + k, count), lax.rem(me - k + count, count)),
            )


def pick(value, index, dim=0):
    return lax.dynamic_index_in_dim(value, index, dim, keepdims=False)


def gather_seq(block):
    count, me = lax.axis_size("seq"), lax.axis_index("seq")
    zeros = (0,) * block.ndim
    column = jnp.zeros((count,) + block.shape, block.dtype)
    column = lax.dynamic_update_slice(column, block[None], (me,) + zeros)
    for pairs, met in steps(count):
        came = lax.ppermute(block, "seq", pairs)
        column = lax.dynamic_update_slice(column, came[None], (met(me)[1],) + zeros)
    return column


def gather_yx(column):
    me = lax.axis_index("yx")
    pieces = [(column, me)]
    for pairs, met in steps(lax.axis_size("yx")):
        pieces.append((lax.ppermute(column, "yx", pairs), met(me)[1]))
    return pieces


def gather_core(pieces):
    count, me = lax.axis_size("core"), lax.axis_index("core")
    shape = pieces[0][0].shape
    zeros = (0,) * len(shape)
    whole = jnp.zeros((len(pieces), count) + shape, pieces[0][0].dtype)
    for piece, place in pieces:
        whole = lax.dynamic_update_slice(whole, piece[None, None], (place, me) + zeros)
        for pairs, met in steps(count):
            other = lax.ppermute(piece, "core", pairs)
            whole = lax.dynamic_update_slice(whole, other[None, None], (place, met(me)[1]) + zeros)
    return whole.reshape((-1,) + shape[1:])


def after(value, *earlier):
    return lax.optimization_barrier((value,) + earlier)[0]


def exchange_sum(pieces, axis):
    me = lax.axis_index(axis)
    total = pick(pieces, me).astype(F32)
    for pairs, met in steps(lax.axis_size(axis)):
        total = total + lax.ppermute(pick(pieces, met(me)[0]), axis, pairs).astype(F32)
    return total


def scatter_sum(value):
    total = exchange_sum(value.swapaxes(0, 1), "core").astype(BF16)
    total = exchange_sum(total, "yx").astype(BF16)
    return exchange_sum(total, "seq")


def local(
    tokens,
    doc_lengths,
    query_weight,
    key_weight,
    value_weight,
    out_weight,
    pool_weight,
    first_gain,
    first_shift,
    inner_weight,
    inner_bias,
    outer_weight,
    outer_bias,
    second_gain,
    second_shift,
    cotangent,
):
    seq_count = lax.axis_size("seq")
    yx_count = lax.axis_size("yx")
    core_count = lax.axis_size("core")
    units = yx_count * core_count
    parts = units * seq_count
    seq_place = lax.axis_index("seq")
    seqs, group, width = tokens.shape
    ff = inner_weight.shape[1]
    panels = ff // width
    share = query_weight.shape[0]
    count = seqs * group
    ext = group + 2 * HALO + PAD

    def shift(value, by):
        pairs = [(i, i + by) for i in range(seq_count) if 0 <= i + by < seq_count]
        return lax.ppermute(value, "seq", pairs)

    vectors = jnp.concatenate(
        (
            pool_weight.reshape(-1),
            first_gain,
            first_shift,
            inner_bias,
            outer_bias,
            second_gain,
            second_shift,
        )
    )
    small_rows = -(-vectors.shape[0] // width)
    small_rows += -(3 * share + small_rows) % 8
    vectors_row = jnp.pad(vectors, (0, small_rows * width - vectors.shape[0])).reshape(small_rows, width)
    early = jnp.concatenate((query_weight, key_weight, value_weight, vectors_row), axis=0)
    late = jnp.concatenate(
        (
            outer_weight,
            inner_weight.reshape(share, panels, width).transpose(1, 0, 2).reshape(-1, width),
            out_weight,
        ),
        axis=0,
    )
    early_column = gather_seq(early)
    late_column = gather_seq(after(late, early_column))
    early_pieces = gather_yx(early_column)
    early = gather_core(early_pieces)
    sent = after(tokens, late_column)
    outer_rows = panels * share
    late_column = jnp.concatenate(
        (
            late_column[:, :outer_rows].reshape(-1, width),
            late_column[:, outer_rows:]
            .reshape(seq_count, panels + 1, share, width)
            .swapaxes(0, 1)
            .reshape(-1, width),
        ),
        axis=0,
    )
    late = lax.all_gather(late_column, ("yx", "core"), axis=0)
    late = late.reshape(units, 2 * panels + 1, seq_count * share, width)
    w_query, w_key, w_value = (
        early[:, i * share : (i + 1) * share].reshape(width, width) for i in range(3)
    )
    small = early[:, 3 * share :].reshape(parts, -1)
    taps = small[:, : 10 * share].reshape(parts, 10, share).transpose(1, 0, 2).reshape(10, width)
    taps = jnp.pad(taps.astype(F32), ((0, 6), (0, 0)))
    at = 10 * share
    vector_list = []
    for size in (share, share, ff // parts, share, share, share):
        vector_list.append(small[:, at : at + size].reshape(1, -1).astype(F32))
        at += size
    gain_one, shift_one, bias_inner, bias_outer, gain_two, shift_two = vector_list
    small_rows_f32 = jnp.concatenate(
        (gain_one, shift_one, bias_outer, gain_two, shift_two, jnp.zeros((3, width), F32)), axis=0
    )
    bias_inner = bias_inner.reshape(panels, 1, width)

    from_left = shift(sent[:, group - HALO :], 1)
    from_right = shift(sent[:, :HALO], -1)
    beyond = shift(sent[:, :1], -2)
    x_ext = jnp.concatenate(
        (from_left, tokens, from_right, jnp.pad(beyond, ((0, 0), (0, PAD - 1), (0, 0)))), axis=1
    )
    flat = tokens.reshape(count, width)
    flat_ext = x_ext.reshape(seqs * ext, width)
    bias, same, slots = masks(doc_lengths, seq_place * group, group, group * seq_count)

    queries = nn(flat, w_query).astype(BF16).reshape(seqs, group, width)
    keys = nn(flat_ext, w_key).astype(BF16).reshape(seqs, ext, width)
    values = nn(flat_ext, w_value).astype(BF16).reshape(seqs, ext, width)
    mixed, lse = attention_forward(queries, keys, values, taps, same, bias)
    core = lax.axis_index("core")
    y, d_first, d_mixed, d_small, d_bias, *d_late = feed_forward(
        core.astype(jnp.int32).reshape(1),
        flat,
        mixed.reshape(count, width),
        cotangent.reshape(count, width),
        small_rows_f32,
        bias_inner,
        late,
    )
    swap = [(0, 1), (1, 0)]
    came = [lax.ppermute(part, "core", swap) for part in d_late[1::2]]
    back = (queries, keys, values, taps, same, bias, lse)
    d_mixed = d_mixed.reshape(seqs, group, width)
    half = seqs // 2
    d_half = attention_backward(*back, after(d_mixed, *d_late), 0, half, ())
    d_late = [
        (mine.astype(F32) + other.astype(F32)).astype(BF16).reshape(yx_count, -1, width)
        for mine, other in zip(d_late[0::2], after(tuple(came), *d_half))
    ]
    d_late = jnp.concatenate(d_late[::-1], axis=1)
    late_sum = lax.psum_scatter(d_late.reshape(-1, width), "yx", scatter_dimension=0, tiled=True)
    d_queries, d_keys, d_values, d_taps = attention_backward(
        *back, after(d_mixed, d_late), half, seqs - half, d_half
    )
    outer_all = seq_count * outer_rows
    late_sum = jnp.concatenate(
        (
            late_sum[:outer_all].reshape(seq_count, outer_rows, width),
            late_sum[outer_all:]
            .reshape(panels + 1, seq_count, share, width)
            .swapaxes(0, 1)
            .reshape(seq_count, (panels + 1) * share, width),
        ),
        axis=1,
    )
    late_sum = exchange_sum(late_sum, "seq")
    d_queries = d_queries.reshape(count, width)
    d_keys = d_keys.reshape(seqs * ext, width)
    d_values = d_values.reshape(seqs * ext, width)
    d_ext = (nt(d_keys, w_key) + nt(d_values, w_value)).reshape(seqs, ext, width)
    right = HALO + group
    to_left = shift(d_ext[:, :HALO].astype(BF16), -1).astype(F32)
    to_right = shift(d_ext[:, right : right + HALO].astype(BF16), 1).astype(F32)
    to_beyond = shift(d_ext[:, right + HALO : right + HALO + 1].astype(BF16), 2).astype(F32)
    d_query_weight = tn(flat, d_queries).astype(BF16)
    d_key_weight = tn(flat_ext, d_keys).astype(BF16)
    d_value_weight = tn(flat_ext, d_values).astype(BF16)
    d_own = nt(d_queries, w_query) + d_first
    d_input = d_own.reshape(seqs, group, width) + d_ext[:, HALO:right]
    d_input = d_input + jnp.pad(to_left, ((0, 0), (group - HALO, 0), (0, 0)))
    d_input = d_input + jnp.pad(to_right, ((0, 0), (0, group - HALO), (0, 0)))
    d_input = d_input + jnp.pad(to_beyond, ((0, 0), (0, group - 1), (0, 0)))

    d_taps = jnp.sum(d_taps, axis=0)[:10]
    d_vectors = jnp.concatenate(
        [d_taps.reshape(10, parts, share).transpose(1, 0, 2).reshape(parts, 10 * share)]
        + [
            piece.reshape(parts, -1)
            for piece in (d_small[0], d_small[1], d_bias, d_small[2], d_small[3], d_small[4])
        ],
        axis=1,
    )
    d_vectors = jnp.pad(d_vectors, ((0, 0), (0, small_rows * width - d_vectors.shape[1])))
    early_grads = jnp.concatenate(
        [g.reshape(parts, share, width) for g in (d_query_weight, d_key_weight, d_value_weight)]
        + [d_vectors.astype(BF16).reshape(parts, small_rows, width)],
        axis=1,
    )
    early_sum = scatter_sum(early_grads.reshape(yx_count, core_count, seq_count, -1, width))

    vector_sum = early_sum[3 * share :].reshape(-1)
    pieces = []
    at = 10 * share
    for size in (share, share, ff // parts, share, share, share):
        pieces.append(vector_sum[at : at + size])
        at += size
    return (
        y.reshape(seqs, group, width),
        d_input.astype(BF16),
        early_sum[:share],
        early_sum[share : 2 * share],
        early_sum[2 * share : 3 * share],
        late_sum[2 * outer_rows :],
        vector_sum[: 10 * share].reshape(10, share),
        pieces[0],
        pieces[1],
        late_sum[outer_rows : 2 * outer_rows]
        .reshape(panels, share, width)
        .transpose(1, 0, 2)
        .reshape(share, ff),
        pieces[2],
        late_sum[:outer_rows],
        pieces[3],
        pieces[4],
        pieces[5],
    )


def solution(mesh):
    dp, seq = mesh.devices.shape
    cores = 2 if dp % 2 == 0 else 1
    mesh = Mesh(mesh.devices.reshape(dp // cores, cores, seq), ("yx", "core", "seq"))
    every = ("yx", "core", "seq")
    rows = P(every, None)
    vector = P(every)
    whole = P(("yx", "core"), "seq", None)
    taps = P(None, every)
    weights = (rows, rows, rows, rows, taps, vector, vector, rows, vector, rows, vector, vector, vector)
    return jax.shard_map(
        local,
        mesh=mesh,
        in_specs=(whole, P(("yx", "core"), None)) + weights + (whole,),
        out_specs=(whole, whole) + weights,
        check_vma=False,
    )
```

time: 578 us -> 390 us (0.67)
  waiting for transfers between devices: 284 us -> 112 us
  Pallas kernels: 125 us -> 97.3 us
  starting transfers between devices: 16.4 us -> 36.3 us
    reduce_scatter x2 -> x1, waiting for transfers between devices: 168 us -> 0.02 us  [local(): lax.psum_scatter(d_late.reshape(-1, width), 'yx', scatter_dimension=0, ti...]
    ppermute x0 -> x26, waiting for transfers between devices: none -> 103 us  [the longest x10 49.6 us: exchange_sum(): lax.ppermute(pick(pieces, met(me)[0]), axis, pairs).astype(F32)]
    ppermute x6, waiting for transfers between devices: 86.5 us -> 8.74 us  [shift(): return lax.ppermute(value, 'seq', pairs)]
    all_gather x2 -> x1, waiting for transfers between devices: 29.5 us -> 0.01 us  [local(): late = lax.all_gather(late_column, ('yx', 'core'), axis=0)]
    ppermute x0 -> x26, starting transfers between devices: none -> 21.4 us  [the longest x10 9.61 us: exchange_sum(): lax.ppermute(pick(pieces, met(me)[0]), axis, pairs).astype(F32)]
    pallas_call x2 -> x3, Pallas kernels: 64.3 us -> 46.2 us  [the longest x2 31.2 us: attention_backward(): pl.pallas_call(kernel, grid=(count,), in_specs=attention_specs(ext, group...]
    dynamic_update_slice x0 -> x16, local copies, waits for them, and re-layouts: none -> 12.5 us  [the longest x4 5.39 us: gather_core(): lax.dynamic_update_slice(whole, piece[None, None], (place, me) + zeros)]
    pallas_call x1, Pallas kernels: 60.5 us -> 51.1 us  [feed_forward(): pl.pallas_call(functools.partial(ffn_kernel, panels), grid=(2 * panels,),...]
  transfers between devices with their start and end apart: 10 -> 34, of which waited for: 7 -> 17; matrix products, arithmetic and copies ran while one was open for 13% -> 25% of each run, Pallas kernels for 5% -> 12%
where the time goes in v2:
time: 390 us; the launch traced here: 385 us
  waiting for transfers between devices  112 us (29%)
  Pallas kernels  97.3 us (25%)
  local copies, waits for them, and re-layouts  58.9 us (15%)
  matrix products  47.2 us (12%)
  starting transfers between devices  36.3 us (9%)
  other arithmetic  18.4 us (5%)
  between operations  15.2 us (4%)
    pallas_call x1, Pallas kernels, feed_forward(): pl.pallas_call(functools.partial(ffn_kernel, panels), grid=(2 * panels,),...  51.1 us
    ppermute x10, waiting for transfers between devices, exchange_sum(): lax.ppermute(pick(pieces, met(me)[0]), axis, pairs).astype(F32)  49.6 us
    ppermute x6, waiting for transfers between devices, gather_seq(): came = lax.ppermute(block, 'seq', pairs)  33.5 us
    pallas_call x2, Pallas kernels, attention_backward(): pl.pallas_call(kernel, grid=(count,), in_specs=attention_specs(ext, group...  31.2 us
    ppermute x3, waiting for transfers between devices, gather_yx(): pieces.append((lax.ppermute(column, 'yx', pairs), met(me)[1]))  19.8 us
    dot_general x3, matrix products, tn(): lax.dot_general(left, right, (((0,), (0,)), ((), ())), preferred_element_...  16.8 us
    dot_general x3, matrix products, nn(): lax.dot_general(left, right, (((1,), (0,)), ((), ())), preferred_element_...  15.6 us
    pallas_call x1, Pallas kernels, attention_forward(): pl.pallas_call(attn_fwd_kernel, grid=(seqs,), in_specs=attention_specs(ex...  15 us
  transfers between devices with their start and end apart: 34, of which 17 were waited for; matrix products, arithmetic and copies ran while one was open for 25% of the time, Pallas kernels for 12%

profile of v2, /device:TPU:16, one launch (start us, length us, event | category | flops | bytes accessed | tf_op | source)
XLA Modules:
  0.0 384.9 jit_solution(13960640057193652165)
XLA Ops:
  8.8 4.1 %concatenate.52 = bf16[456]{0:T(512)(128)(2,1)S(1)} concatenate(bf16[240]{0:T(256)(128)(2,1)S(1)} %reshape.402, bf16[24]{0:T(256)(128)(2,1)} %param.23, bf16[24]{0:T(256)(128)(2,1)} %param.24, bf16[96]{0:T(256)(128)(2,1)} %param.26, bf16[24]{0:T(256)(128)(2,1)} %param.28, bf16[24]{0:T(256)(128)(2,1)} %param.29, bf16[24]{0:T(256)(128)(2,1)} %param.30), dimensions={0} | concatenate | bytes 1824 | tf_op jit(solution)/shard_map/concatenate | solution.py:674
  14.5 1.6 collective-permute-start
  16.4 1.6 collective-permute-start.2
  22.0 3.3 collective-permute-done.1
  26.0 2.7 collective-permute-done.2
  30.0 1.2 collective-permute-start.11
  31.2 1.6 collective-permute-start.12
  32.9 7.8 %collective-permute-done.10 = bf16[216,768]{1,0:T(8,128)(2,1)S(1)} collective-permute-done((bf16[216,768]{1,0:T(8,128)(2,1)S(1)}, bf16[216,768]{1,0:T(8,128)(2,1)S(1)}, u32[]{:S(2)}, u32[]{:S(2)}) %collective-permute-start.10) | collective-permute-done | bytes 331808 | tf_op jit(solution)/shard_map/ppermute | solution.py:595
  40.8 12.9 %collective-permute-done.11 = bf16[216,768]{1,0:T(8,128)(2,1)S(1)} collective-permute-done((bf16[216,768]{1,0:T(8,128)(2,1)S(1)}, bf16[216,768]{1,0:T(8,128)(2,1)S(1)}, u32[]{:S(2)}, u32[]{:S(2)}) %collective-permute-start.11) | collective-permute-done | bytes 331808 | tf_op jit(solution)/shard_map/ppermute | solution.py:595
  53.7 6.7 %collective-permute-done.12 = bf16[216,768]{1,0:T(8,128)(2,1)S(1)} collective-permute-done((bf16[216,768]{1,0:T(8,128)(2,1)S(1)}, bf16[216,768]{1,0:T(8,128)(2,1)S(1)}, u32[]{:S(2)}, u32[]{:S(2)}) %collective-permute-start.12) | collective-permute-done | bytes 331808 | tf_op jit(solution)/shard_map/ppermute | solution.py:595
  60.7 1.1 pad_maximum_fusion.3
  64.8 1.6 collective-permute-start.4
  66.5 1.6 collective-permute-start.6
  68.6 2.3 broadcast_in_dim.120
  70.9 1.9 bitcast_dynamic-update-slice_fusion.7
  72.8 1.9 collective-permute-start.13
  75.5 3.9 %collective-permute-start.14 = (bf16[4,256,768]{2,1,0:T(8,128)(2,1)}, bf16[4,256,768]{2,1,0:T(8,128)(2,1)}, u32[]{:S(2)}, u32[]{:S(2)}) collective-permute-start(bf16[4,256,768]{2,1,0:T(8,128)(2,1)} %param.16), channel_id=1, source_target_pairs={{1,0},{2,1},{3,2},{5,4},{6,5},{7,6},{9,8},{10,9},{11,10},{13,12},{... | collective-permute-start | bytes 4718600 | tf_op jit(solution)/shard_map/ppermute | solution.py:672
  79.4 5.9 %collective-permute-done.4 = bf16[4,80,768]{2,1,0:T(8,128)(2,1)} collective-permute-done((bf16[4,80,768]{2,1,0:T(8,128)(2,1)}, bf16[4,80,768]{2,1,0:T(8,128)(2,1)}, u32[]{:S(2)}, u32[]{:S(2)}) %collective-permute-start.4) | collective-permute-done | bytes 491552 | tf_op jit(solution)/shard_map/ppermute | solution.py:604
  85.3 1.9 bitcast_dynamic-update-slice_fusion.6
  87.2 1.9 bitcast_dynamic-update-slice_fusion.5
  89.0 1.9 collective-permute-done.6
  90.9 1.5 collective-permute-start.15
  92.3 12.1 %collective-permute-done.8 = bf16[4,80,768]{2,1,0:T(8,128)(2,1)S(1)} collective-permute-done((bf16[4,80,768]{2,1,0:T(8,128)(2,1)}, bf16[4,80,768]{2,1,0:T(8,128)(2,1)S(1)}, u32[]{:S(2)}, u32[]{:S(2)}) %collective-permute-start.8) | collective-permute-done | bytes 491552 | tf_op jit(solution)/shard_map/ppermute | solution.py:604
  110.8 3.8 fusion.26
  114.6 4.4 %fusion.7 = bf16[1024,768]{0,1:T(8,128)(2,1)} fusion(bf16[768,768]{1,0:T(8,128)(2,1)S(1)} %bitcast.197, bf16[1024,768]{1,0:T(8,128)(2,1)} %bitcast.1.x_ref), kind=kOutput, calls=%fused_computation.32 | convolution fusion | flops 1208745984 | bytes 4325376 | tf_op jit(solution)/shard_map/dot_general | solution.py:42
  119.5 1.8 copy.105
  122.6 3.3 fusion.1
  126.0 5.6 %convolution_convert_fusion = bf16[3136,768]{1,0:T(8,128)(2,1)} fusion(bf16[3136,768]{1,0:T(8,128)(2,1)S(1)} %bitcast.189, bf16[768,768]{1,0:T(8,128)(2,1)S(1)} %bitcast.207), kind=kOutput, calls=%fused_computation.3 | convolution fusion | flops 3701784576 | bytes 10813440 | tf_op jit(solution)/shard_map/dot_general | solution.py:42
  131.6 5.5 %convolution_convert_fusion.1 = bf16[3136,768]{1,0:T(8,128)(2,1)} fusion(bf16[3136,768]{1,0:T(8,128)(2,1)S(1)} %bitcast.190, bf16[768,768]{1,0:T(8,128)(2,1)S(1)} %bitcast.209), kind=kOutput, calls=%fused_computation.4 | convolution fusion | flops 3701784576 | bytes 10813440 | tf_op jit(solution)/shard_map/dot_general | solution.py:42
  137.1 1.9 broadcast_in_dim.144.same_ref.refs_4_
  139.0 15.0 %attn_fwd.1 = (bf16[4,256,768]{2,1,0:T(8,128)(2,1)S(1)}, f32[4,6,2,256]{3,2,1,0:T(2,128)S(1)}) custom-call(bf16[4,256,768]{2,1,0:T(8,128)(2,1)S(1)} %bitcast.164, bf16[4,784,768]{2,1,0:T(8,128)(2,1)} %bitcast.177, bf16[4,784,768]{2,1,0:T(8,128)(2,1)} %bitcast.174, f32[16,768]{1,0:T(8,128)S(1)} %pad_convert_fusion.w_ref.refs_3_, ...), custom_call_target="tpu_custom_call" | custom-call | flops 1048576 | bytes 1048576 | tf_op jit(solution)/shard_map/attn_fwd/pallas_call | solution.py:240
  155.2 51.1 %ffn.1 = (bf16[1024,768]{1,0:T(8,128)(2,1)}, f32[1024,768]{1,0:T(8,128)}, bf16[1024,768]{1,0:T(8,128)(2,1)}, f32[8,768]{1,0:T(8,128)}, f32[4,1,768]{2,1,0:T(1,12...) custom-call(s32[1]{0:T(128)} %bitcast.core_ref, ...), custom_call_target="tpu_custom_call" | custom-call | flops 1048576 | bytes 1048576 | tf_op jit(solution)/shard_map/ffn/pallas_call | solution.py:482
  206.9 1.4 copy-done.1
  209.2 15.7 %attn_bwd.2 = (bf16[4,256,768]{2,1,0:T(8,128)(2,1)S(1)}, bf16[4,784,768]{2,1,0:T(8,128)(2,1)}, bf16[4,784,768]{2,1,0:T(8,128)(2,1)}, f32[4,16,768]{2,1,0:T(8,128)S(1)}) custom-call(bf16[4,256,768]{2,1,0:T(8,128)(2,1)S(1)} %bitcast.165, bf16[4,784,768]{2,1,0:T(8,128)(2,1)} %bitcast.178, bf16[4,784,768]{2,1,0:T(8,128)(2,1)} %bitcast.175, ...), custom_call_target="tpu_custom_call" | custom-call | flops 1048576 | bytes 1048576 | tf_op jit(solution)/shard_map/attn_bwd/pallas_call | solution.py:270
  227.7 2.9 pad_maximum_fusion
  233.3 1.4 copy-done.2
  234.7 15.5 %attn_bwd.3 = (bf16[4,256,768]{2,1,0:T(8,128)(2,1)S(1)}, bf16[4,784,768]{2,1,0:T(8,128)(2,1)}, bf16[4,784,768]{2,1,0:T(8,128)(2,1)}, f32[4,16,768]{2,1,0:T(8,128)S(1)}) custom-call(bf16[4,256,768]{2,1,0:T(8,128)(2,1)S(1)} %bitcast.166, bf16[4,784,768]{2,1,0:T(8,128)(2,1)} %bitcast.179, ...), custom_call_target="tpu_custom_call", output_to_operand_aliasing={{0}: (8, {}), {1}: (9, {}), {2}: (10, {}), {3}: (11, {})} | custom-call | flops 1048576 | bytes 1048576 | tf_op jit(solution)/shard_map/attn_bwd/pallas_call | solution.py:270
  251.6 3.1 bitcast_convert_fusion.2
  254.7 7.0 %bitcast_convert_fusion.1 = bf16[768,768]{1,0:T(8,128)(2,1)S(1)} fusion(bf16[4,784,768]{2,1,0:T(8,128)(2,1)S(1)} %bitcast.192, bf16[4,1,768]{2,1,0:T(2,128)(2,1)S(1)} %copy-done.18, bf16[4,256,768]{2,1,0:T(8,128)(2,1)} %collective-permute-done.14, bf16[4,256,768]{2,1,0:T(8,128)(2,1)} %param.16, bf16[4,256,768]{2,1,0:T(8,128)(2,1)} %collective-permute-done.13), kind=kOutput, calls=%fused_computation.18 | convolution fusion | flops 3724050432 | bytes 10721280 | tf_op jit(solution)/shard_map/dot_general | solution.py:38
  261.8 6.6 %bitcast_convert_fusion = bf16[768,768]{1,0:T(8,128)(2,1)S(1)} fusion(bf16[4,784,768]{2,1,0:T(8,128)(2,1)S(1)} %bitcast.195, bf16[4,1,768]{2,1,0:T(2,128)(2,1)S(1)} %copy-done.18, bf16[4,256,768]{2,1,0:T(8,128)(2,1)} %collective-permute-done.14, bf16[4,256,768]{2,1,0:T(8,128)(2,1)} %param.16, bf16[4,256,768]{2,1,0:T(8,128)(2,1)} %collective-permute-done.13), kind=kOutput, calls=%fused_computation.17 | convolution fusion | flops 3724050432 | bytes 10721280 | tf_op jit(solution)/shard_map/dot_general | solution.py:38
  268.8 1.4 dynamic-slice_bitcast_fusion
  270.7 6.4 %fusion.33 = f32[3136,768]{1,0:T(8,128)} fusion(bf16[3136,768]{1,0:T(8,128)(2,1)S(1)} %bitcast.193, bf16[768,768]{1,0:T(8,128)(2,1)S(1)} %bitcast.210), kind=kOutput, calls=%fused_computation.128 | convolution fusion | flops 3699376128 | bytes 15630336 | tf_op jit(solution)/shard_map/dot_general | solution.py:34
  277.1 6.9 %convolution_add_fusion = f32[3136,768]{1,0:T(8,128)S(1)} fusion(f32[3136,768]{1,0:T(8,128)} %fusion.33, bf16[3136,768]{1,0:T(8,128)(2,1)S(1)} %bitcast.196, bf16[768,768]{1,0:T(8,128)(2,1)S(1)} %bitcast.208), kind=kOutput, calls=%fused_computation.2 | convolution fusion | flops 3701784576 | bytes 25264128 | tf_op jit(solution)/shard_map/dot_general | solution.py:34
  284.0 2.7 convert.58
  286.7 2.1 fusion.25
  288.8 2.5 collective-permute-start.19
  291.3 3.7 collective-permute-start.20
  295.7 1.5 collective-permute-start.23
  297.2 1.2 collective-permute-start.24
  300.1 1.5 convolution_add_fusion.1
  301.6 8.4 %collective-permute-done.23 = bf16[4,80,768]{2,1,0:T(8,128)(2,1)S(1)} collective-permute-done((bf16[4,80,768]{2,1,0:T(8,128)(2,1)S(1)}, bf16[4,80,768]{2,1,0:T(8,128)(2,1)S(1)}, u32[]{:S(2)}, u32[]{:S(2)}) %collective-permute-start.23) | collective-permute-done | bytes 491552 | tf_op jit(solution)/shard_map/ppermute | solution.py:629
  309.9 1.3 collective-permute-start.21
  311.2 8.9 %collective-permute-done.24 = bf16[4,80,768]{2,1,0:T(8,128)(2,1)S(1)} collective-permute-done((bf16[4,80,768]{2,1,0:T(8,128)(2,1)S(1)}, bf16[4,80,768]{2,1,0:T(8,128)(2,1)S(1)}, u32[]{:S(2)}, u32[]{:S(2)}) %collective-permute-start.24) | collective-permute-done | bytes 491552 | tf_op jit(solution)/shard_map/ppermute | solution.py:629
  320.5 1.9 collective-permute-start.27
  322.4 7.9 %collective-permute-done.21 = bf16[4,1,768]{2,1,0:T(2,128)(2,1)S(1)} collective-permute-done((bf16[4,1,768]{2,1,0:T(2,128)(2,1)S(1)}, bf16[4,1,768]{2,1,0:T(2,128)(2,1)S(1)}, u32[]{:S(2)}, u32[]{:S(2)}) %collective-permute-start.21) | collective-permute-done | bytes 6176 | tf_op jit(solution)/shard_map/ppermute | solution.py:672
  331.6 2.1 fusion.6
  333.6 2.1 collective-permute-done.27
  335.7 4.9 %collective-permute-done.28 = bf16[80,768]{1,0:T(8,128)(2,1)S(1)} collective-permute-done((bf16[80,768]{1,0:T(8,128)(2,1)S(1)}, bf16[80,768]{1,0:T(8,128)(2,1)S(1)}, u32[]{:S(2)}, u32[]{:S(2)}) %collective-permute-start.28) | collective-permute-done | bytes 122912 | tf_op jit(solution)/shard_map/ppermute | solution.py:629
  340.8 1.2 slice.254
  344.3 2.5 collective-permute-start.31
  349.3 5.3 %collective-permute-done.29 = bf16[216,768]{1,0:T(8,128)(2,1)S(1)} collective-permute-done((bf16[216,768]{1,0:T(8,128)(2,1)S(1)}, bf16[216,768]{1,0:T(8,128)(2,1)S(1)}, u32[]{:S(2)}, u32[]{:S(2)}) %collective-permute-start.29) | collective-permute-done | bytes 331808 | tf_op jit(solution)/shard_map/ppermute | solution.py:629
  354.7 12.1 %collective-permute-done.30 = bf16[216,768]{1,0:T(8,128)(2,1)S(1)} collective-permute-done((bf16[216,768]{1,0:T(8,128)(2,1)S(1)}, bf16[216,768]{1,0:T(8,128)(2,1)S(1)}, u32[]{:S(2)}, u32[]{:S(2)}) %collective-permute-start.30) | collective-permute-done | bytes 331808 | tf_op jit(solution)/shard_map/ppermute | solution.py:629
  366.7 7.9 %collective-permute-done.31 = bf16[216,768]{1,0:T(8,128)(2,1)} collective-permute-done((bf16[216,768]{1,0:T(8,128)(2,1)S(1)}, bf16[216,768]{1,0:T(8,128)(2,1)}, u32[]{:S(2)}, u32[]{:S(2)}) %collective-permute-start.31) | collective-permute-done | bytes 331808 | tf_op jit(solution)/shard_map/ppermute | solution.py:629
  374.6 1.1 fusion.12
  (207 shorter events, 43.5 us)
Async XLA Ops:
  7.2 148.0 %all-gather.3.cloned.1.call-start = ((), (), s32[]{:S(2)}) async-start(), calls=%async_computation.2 | async-start | bytes 11943936 | tf_op jit(solution)/shard_map/all_gather | solution.py:713
  14.5 6.9 %collective-permute-start = (bf16[80,768]{1,0:T(8,128)(2,1)S(1)}, bf16[80,768]{1,0:T(8,128)(2,1)S(1)}, u32[]{:S(2)}, u32[]{:S(2)}) collective-permute-start(bf16[80,768]{1,0:T(8,128)(2,1)S(1)} %constant_dynamic-update-slice_fusion), channel_id=1, source_target_pairs={{0,1},{1,0},{2,3},{3,2},{4,5},{5,4},{6,7},{7,6},{8,9},{9,8},{10,11... | collective-permute-start | bytes 368648 | tf_op jit(solution)/shard_map/ppermute | solution.py:595
  16.1 9.3 %collective-permute-start.1 = (bf16[80,768]{1,0:T(8,128)(2,1)S(1)}, bf16[80,768]{1,0:T(8,128)(2,1)S(1)}, u32[]{:S(2)}, u32[]{:S(2)}) collective-permute-start(bf16[80,768]{1,0:T(8,128)(2,1)S(1)} %constant_dynamic-update-slice_fusion), channel_id=1, source_target_pairs={{0,2},{1,3},{2,0},{3,1},{4,6},{5,7},{6,4},{7,5},{8,10},{9,11},{10,... | collective-permute-start | bytes 368648 | tf_op jit(solution)/shard_map/ppermute | solution.py:595
  16.4 12.3 %collective-permute-start.2 = (bf16[80,768]{1,0:T(8,128)(2,1)S(1)}, bf16[80,768]{1,0:T(8,128)(2,1)S(1)}, u32[]{:S(2)}, u32[]{:S(2)}) collective-permute-start(bf16[80,768]{1,0:T(8,128)(2,1)S(1)} %constant_dynamic-update-slice_fusion), channel_id=1, source_target_pairs={{0,3},{1,2},{2,1},{3,0},{4,7},{5,6},{6,5},{7,4},{8,11},{9,10},{10,... | collective-permute-start | bytes 368648 | tf_op jit(solution)/shard_map/ppermute | solution.py:595
  29.3 11.5 %collective-permute-start.10 = (bf16[216,768]{1,0:T(8,128)(2,1)S(1)}, bf16[216,768]{1,0:T(8,128)(2,1)S(1)}, u32[]{:S(2)}, u32[]{:S(2)}) collective-permute-start(bf16[216,768]{1,0:T(8,128)(2,1)S(1)} %pad_maximum_fusion.4), channel_id=1, source_target_pairs={{0,1},{1,0},{2,3},{3,2},{4,5},{5,4},{6,7},{7,6},{8,9},{9,8},{10,11... | collective-permute-start | bytes 995336 | tf_op jit(solution)/shard_map/ppermute | solution.py:595
  30.0 23.7 %collective-permute-start.11 = (bf16[216,768]{1,0:T(8,128)(2,1)S(1)}, bf16[216,768]{1,0:T(8,128)(2,1)S(1)}, u32[]{:S(2)}, u32[]{:S(2)}) collective-permute-start(bf16[216,768]{1,0:T(8,128)(2,1)S(1)} %pad_maximum_fusion.4), channel_id=1, source_target_pairs={{0,2},{1,3},{2,0},{3,1},{4,6},{5,7},{6,4},{7,5},{8,10},{9,11},{10,... | collective-permute-start | bytes 995336 | tf_op jit(solution)/shard_map/ppermute | solution.py:595
  31.2 29.2 %collective-permute-start.12 = (bf16[216,768]{1,0:T(8,128)(2,1)S(1)}, bf16[216,768]{1,0:T(8,128)(2,1)S(1)}, u32[]{:S(2)}, u32[]{:S(2)}) collective-permute-start(bf16[216,768]{1,0:T(8,128)(2,1)S(1)} %pad_maximum_fusion.4), channel_id=1, source_target_pairs={{0,3},{1,2},{2,1},{3,0},{4,7},{5,6},{6,5},{7,4},{8,11},{9,10},{10,... | collective-permute-start | bytes 995336 | tf_op jit(solution)/shard_map/ppermute | solution.py:595
  60.5 1.4 copy-start.21
  60.6 3.3 copy-start.20
  61.9 278.9 %reduce-scatter.2.cloned.1.call-start = ((), (), s32[]{:S(2)}) async-start(), calls=%async_computation.1 | async-start | bytes 6635520 | tf_op jit(solution)/shard_map/reduce_scatter | solution.py:767
  64.7 10.8 %collective-permute-start.3 = (bf16[4,80,768]{2,1,0:T(8,128)(2,1)}, bf16[4,80,768]{2,1,0:T(8,128)(2,1)}, u32[]{:S(2)}, u32[]{:S(2)}) collective-permute-start(bf16[4,80,768]{2,1,0:T(8,128)(2,1)} %bitcast_dynamic-update-slice_fusion.12), channel_id=1, source_target_pairs={{0,4},{4,0},{1,5},{5,1},{2,6},{6,2},{3,7},{7,3},{8,12},{12,8},{9,1... | collective-permute-start | bytes 1474568 | tf_op jit(solution)/shard_map/ppermute | solution.py:616
  64.8 20.5 %collective-permute-start.4 = (bf16[4,80,768]{2,1,0:T(8,128)(2,1)}, bf16[4,80,768]{2,1,0:T(8,128)(2,1)}, u32[]{:S(2)}, u32[]{:S(2)}) collective-permute-start(bf16[4,80,768]{2,1,0:T(8,128)(2,1)} %bitcast_dynamic-update-slice_fusion.12), channel_id=1, source_target_pairs={{0,8},{8,0},{16,24},{24,16},{1,9},{9,1},{17,25},{25,17},{2,10},{10... | collective-permute-start | bytes 1474568 | tf_op jit(solution)/shard_map/ppermute | solution.py:604
  66.5 72.5 %copy-start = (f32[4,2,416,128]{3,2,1,0:T(8,128)}, f32[4,2,416,128]{3,2,1,0:T(8,128)S(1)}, u32[]{:S(2)}) copy-start(f32[4,2,416,128]{3,2,1,0:T(8,128)S(1)} %pad_maximum_fusion.2.bias_ref.refs_5_) | copy-start | bytes 5111812
  66.5 24.3 %collective-permute-start.6 = (bf16[4,80,768]{2,1,0:T(8,128)(2,1)}, bf16[4,80,768]{2,1,0:T(8,128)(2,1)S(1)}, u32[]{:S(2)}, u32[]{:S(2)}) collective-permute-start(bf16[4,80,768]{2,1,0:T(8,128)(2,1)} %bitcast_dynamic-update-slice_fusion.12), channel_id=1, source_target_pairs={{0,16},{8,24},{16,0},{24,8},{1,17},{9,25},{17,1},{25,9},{2,18},{10... | collective-permute-start | bytes 1474568 | tf_op jit(solution)/shard_map/ppermute | solution.py:604
  68.1 36.3 %collective-permute-start.8 = (bf16[4,80,768]{2,1,0:T(8,128)(2,1)}, bf16[4,80,768]{2,1,0:T(8,128)(2,1)S(1)}, u32[]{:S(2)}, u32[]{:S(2)}) collective-permute-start(bf16[4,80,768]{2,1,0:T(8,128)(2,1)} %bitcast_dynamic-update-slice_fusion.12), channel_id=1, source_target_pairs={{0,24},{8,16},{16,8},{24,0},{1,25},{9,17},{17,9},{25,1},{2,26},{10... | collective-permute-start | bytes 1474568 | tf_op jit(solution)/shard_map/ppermute | solution.py:604
  72.8 49.9 %collective-permute-start.13 = (bf16[4,256,768]{2,1,0:T(8,128)(2,1)}, bf16[4,256,768]{2,1,0:T(8,128)(2,1)}, u32[]{:S(2)}, u32[]{:S(2)}) collective-permute-start(bf16[4,256,768]{2,1,0:T(8,128)(2,1)} %param.16), channel_id=1, source_target_pairs={{0,1},{1,2},{2,3},{4,5},{5,6},{6,7},{8,9},{9,10},{10,11},{12,13},{... | collective-permute-start | bytes 4718600 | tf_op jit(solution)/shard_map/ppermute | solution.py:672
  75.5 47.1 %collective-permute-start.14 = (bf16[4,256,768]{2,1,0:T(8,128)(2,1)}, bf16[4,256,768]{2,1,0:T(8,128)(2,1)}, u32[]{:S(2)}, u32[]{:S(2)}) collective-permute-start(bf16[4,256,768]{2,1,0:T(8,128)(2,1)} %param.16), channel_id=1, source_target_pairs={{1,0},{2,1},{3,2},{5,4},{6,5},{7,6},{9,8},{10,9},{11,10},{13,12},{... | collective-permute-start | bytes 4718600 | tf_op jit(solution)/shard_map/ppermute | solution.py:672
  85.3 19.1 %collective-permute-start.5 = (bf16[4,80,768]{2,1,0:T(8,128)(2,1)}, bf16[4,80,768]{2,1,0:T(8,128)(2,1)S(1)}, u32[]{:S(2)}, u32[]{:S(2)}) collective-permute-start(bf16[4,80,768]{2,1,0:T(8,128)(2,1)} %collective-permute-done.4), channel_id=1, source_target_pairs={{0,4},{4,0},{1,5},{5,1},{2,6},{6,2},{3,7},{7,3},{8,12},{12,8},{9,1... | collective-permute-start | bytes 1474568 | tf_op jit(solution)/shard_map/ppermute | solution.py:616
  90.9 31.7 %collective-permute-start.15 = (bf16[4,1,768]{2,1,0:T(2,128)(2,1)S(1)}, bf16[4,1,768]{2,1,0:T(2,128)(2,1)S(1)}, u32[]{:S(2)}, u32[]{:S(2)}) collective-permute-start(bf16[4,1,768]{2,1,0:T(2,128)(2,1)S(1)} %slice.169), channel_id=1, source_target_pairs={{2,0},{3,1},{6,4},{7,5},{10,8},{11,9},{14,12},{15,13},{18,16},{19,... | collective-permute-start | bytes 18440 | tf_op jit(solution)/shard_map/ppermute | solution.py:672
  104.4 2.2 collective-permute-start.7
  104.4 3.9 %collective-permute-start.9 = (bf16[4,80,768]{2,1,0:T(8,128)(2,1)S(1)}, bf16[4,80,768]{2,1,0:T(8,128)(2,1)S(1)}, u32[]{:S(2)}, u32[]{:S(2)}) collective-permute-start(bf16[4,80,768]{2,1,0:T(8,128)(2,1)S(1)} %collective-permute-done.8), channel_id=1, source_target_pairs={{0,4},{4,0},{1,5},{5,1},{2,6},{6,2},{3,7},{7,3},{8,12},{12,8},{9,1... | collective-permute-start | bytes 1474568 | tf_op jit(solution)/shard_map/ppermute | solution.py:616
  114.6 4.4 %copy-start.6 = (bf16[32,24,768]{2,1,0:T(8,128)(2,1)}, bf16[32,24,768]{2,1,0:T(8,128)(2,1)S(1)}, u32[]{:S(2)}) copy-start(bf16[32,24,768]{2,1,0:T(8,128)(2,1)S(1)} %get-tuple-element.80) | copy-start | bytes 3538948
  122.6 3.3 copy-start.11
  122.6 3.3 copy-start.17
  125.9 5.6 %copy-start.13 = (bf16[32,24,768]{2,1,0:T(8,128)(2,1)S(1)}, bf16[32,24,768]{2,1,0:T(8,128)(2,1)}, u32[]{:S(2)}) copy-start(bf16[32,24,768]{2,1,0:T(8,128)(2,1)} %get-tuple-element.79) | copy-start | bytes 3538948
  154.0 1.1 copy-start.3
  155.2 51.1 %copy-start.4 = (f32[4,6,2,256]{3,2,1,0:T(2,128)}, f32[4,6,2,256]{3,2,1,0:T(2,128)S(1)}, u32[]{:S(2)}) copy-start(f32[4,6,2,256]{3,2,1,0:T(2,128)S(1)} %get-tuple-element.47.refs_6_) | copy-start | bytes 147460
  206.3 18.5 %collective-permute-start.17 = (bf16[4,4,96,768]{3,2,1,0:T(8,128)(2,1)}, bf16[4,4,96,768]{3,2,1,0:T(8,128)(2,1)S(1)}, u32[]{:S(2)}, u32[]{:S(2)}) collective-permute-start(bf16[4,4,96,768]{3,2,1,0:T(8,128)(2,1)} %get-tuple-element.51), channel_id=1, source_target_pairs={{0,4},{4,0},{1,5},{5,1},{2,6},{6,2},{3,7},{7,3},{8,12},{12,8},{9,1... | collective-permute-start | bytes 7077896 | tf_op jit(solution)/shard_map/ppermute | solution.py:757
  206.4 18.4 %collective-permute-start.18 = (bf16[4,384,768]{2,1,0:T(8,128)(2,1)}, bf16[4,384,768]{2,1,0:T(8,128)(2,1)S(1)}, u32[]{:S(2)}, u32[]{:S(2)}) collective-permute-start(bf16[4,384,768]{2,1,0:T(8,128)(2,1)} %get-tuple-element.52), channel_id=1, source_target_pairs={{0,4},{4,0},{1,5},{5,1},{2,6},{6,2},{3,7},{7,3},{8,12},{12,8},{9,1... | collective-permute-start | bytes 7077896 | tf_op jit(solution)/shard_map/ppermute | solution.py:757
  206.9 17.9 %collective-permute-start.16 = (bf16[4,96,768]{2,1,0:T(8,128)(2,1)}, bf16[4,96,768]{2,1,0:T(8,128)(2,1)S(1)}, u32[]{:S(2)}, u32[]{:S(2)}) collective-permute-start(bf16[4,96,768]{2,1,0:T(8,128)(2,1)} %get-tuple-element.50), channel_id=1, source_target_pairs={{0,4},{4,0},{1,5},{5,1},{2,6},{6,2},{3,7},{7,3},{8,12},{12,8},{9,1... | collective-permute-start | bytes 1769480 | tf_op jit(solution)/shard_map/ppermute | solution.py:757
  206.9 1.4 copy-start.1
  208.4 0.8 copy-start.5
  209.2 15.7 %copy-start.10 = (bf16[4,384,768]{2,1,0:T(8,128)(2,1)S(1)}, bf16[4,384,768]{2,1,0:T(8,128)(2,1)}, u32[]{:S(2)}) copy-start(bf16[4,384,768]{2,1,0:T(8,128)(2,1)} %get-tuple-element.49) | copy-start | bytes 7077892
  224.8 1.7 copy-start.9
  226.5 1.1 copy-start.15
  230.7 0.7 copy-start.16
  230.7 1.9 copy-start.19
  233.3 1.4 copy-start.2
  251.5 3.2 slice-start
  251.5 3.2 slice-start.1
  251.6 3.2 copy-start.18
  251.6 10.2 %slice-start.2 = ((s8[4816896]{0:T(1024)(128)(4,1)}), s8[4194304]{0:T(1024)(128)(4,1)S(1)}, s32[]{:S(2)}) async-start(s8[4816896]{0:T(1024)(128)(4,1)} %bitcast.194), calls=%async_computation.5 | async-start | bytes 8388608
  254.7 7.1 %slice-start.3 = ((s8[4816896]{0:T(1024)(128)(4,1)}), s8[622592]{0:T(1024)(128)(4,1)S(1)}, s32[]{:S(2)}) async-start(s8[4816896]{0:T(1024)(128)(4,1)} %bitcast.194), calls=%async_computation.6 | async-start | bytes 1245184
  268.8 1.9 copy-start.14
  270.2 24.8 %collective-permute-start.22 = (bf16[4,4,80,768]{3,2,1,0:T(8,128)(2,1)}, bf16[4,4,80,768]{3,2,1,0:T(8,128)(2,1)S(1)}, u32[]{:S(2)}, u32[]{:S(2)}) collective-permute-start(bf16[4,4,80,768]{3,2,1,0:T(8,128)(2,1)} %dynamic-slice_bitcast_fusion), channel_id=1, source_target_pairs={{0,4},{4,0},{1,5},{5,1},{2,6},{6,2},{3,7},{7,3},{8,12},{12,8},{9,1... | collective-permute-start | bytes 5898248 | tf_op jit(solution)/shard_map/ppermute | solution.py:629
  270.7 6.4 %copy-start.12 = (bf16[32,24,768]{2,1,0:T(8,128)(2,1)S(1)}, bf16[32,24,768]{2,1,0:T(8,128)(2,1)}, u32[]{:S(2)}) copy-start(bf16[32,24,768]{2,1,0:T(8,128)(2,1)} %get-tuple-element.78) | copy-start | bytes 3538948
  288.8 42.0 %collective-permute-start.19 = (bf16[4,256,768]{2,1,0:T(8,128)(2,1)S(1)}, bf16[4,256,768]{2,1,0:T(8,128)(2,1)S(1)}, u32[]{:S(2)}, u32[]{:S(2)}) collective-permute-start(bf16[4,256,768]{2,1,0:T(8,128)(2,1)S(1)} %get-tuple-element.76), channel_id=1, source_target_pairs={{1,0},{2,1},{3,2},{5,4},{6,5},{7,6},{9,8},{10,9},{11,10},{13,12},{... | collective-permute-start | bytes 4718600 | tf_op jit(solution)/shard_map/ppermute | solution.py:672
  291.2 8.8 %copy-start.7 = (bf16[32,24,768]{2,1,0:T(8,128)(2,1)S(1)}, bf16[32,24,768]{2,1,0:T(8,128)(2,1)}, u32[]{:S(2)}) copy-start(bf16[32,24,768]{2,1,0:T(8,128)(2,1)} %copy-done.6) | copy-start | bytes 3538948
  291.3 8.8 %copy-start.8 = (f32[1024,768]{1,0:T(8,128)S(1)}, f32[1024,768]{1,0:T(8,128)}, u32[]{:S(2)}) copy-start(f32[1024,768]{1,0:T(8,128)} %get-tuple-element.65) | copy-start | bytes 9437188
  291.3 40.3 %collective-permute-start.20 = (bf16[4,256,768]{2,1,0:T(8,128)(2,1)S(1)}, bf16[4,256,768]{2,1,0:T(8,128)(2,1)S(1)}, u32[]{:S(2)}, u32[]{:S(2)}) collective-permute-start(bf16[4,256,768]{2,1,0:T(8,128)(2,1)S(1)} %get-tuple-element.77), channel_id=1, source_target_pairs={{0,1},{1,2},{2,3},{4,5},{5,6},{6,7},{8,9},{9,10},{10,11},{12,13},{... | collective-permute-start | bytes 4718600 | tf_op jit(solution)/shard_map/ppermute | solution.py:672
  295.7 14.2 %collective-permute-start.23 = (bf16[4,80,768]{2,1,0:T(8,128)(2,1)S(1)}, bf16[4,80,768]{2,1,0:T(8,128)(2,1)S(1)}, u32[]{:S(2)}, u32[]{:S(2)}) collective-permute-start(bf16[4,80,768]{2,1,0:T(8,128)(2,1)S(1)} %get-tuple-element.81), channel_id=1, source_target_pairs={{0,8},{8,0},{16,24},{24,16},{1,9},{9,1},{17,25},{25,17},{2,10},{10... | collective-permute-start | bytes 1474568 | tf_op jit(solution)/shard_map/ppermute | solution.py:629
  297.2 23.0 %collective-permute-start.24 = (bf16[4,80,768]{2,1,0:T(8,128)(2,1)S(1)}, bf16[4,80,768]{2,1,0:T(8,128)(2,1)S(1)}, u32[]{:S(2)}, u32[]{:S(2)}) collective-permute-start(bf16[4,80,768]{2,1,0:T(8,128)(2,1)S(1)} %get-tuple-element.83), channel_id=1, source_target_pairs={{0,16},{8,24},{16,0},{24,8},{1,17},{9,25},{17,1},{25,9},{2,18},{10... | collective-permute-start | bytes 1474568 | tf_op jit(solution)/shard_map/ppermute | solution.py:629
  298.4 21.8 %collective-permute-start.25 = (bf16[4,80,768]{2,1,0:T(8,128)(2,1)S(1)}, bf16[4,80,768]{2,1,0:T(8,128)(2,1)S(1)}, u32[]{:S(2)}, u32[]{:S(2)}) collective-permute-start(bf16[4,80,768]{2,1,0:T(8,128)(2,1)S(1)} %get-tuple-element.82), channel_id=1, source_target_pairs={{0,24},{8,16},{16,8},{24,0},{1,25},{9,17},{17,9},{25,1},{2,26},{10... | collective-permute-start | bytes 1474568 | tf_op jit(solution)/shard_map/ppermute | solution.py:629
  309.9 20.4 %collective-permute-start.21 = (bf16[4,1,768]{2,1,0:T(2,128)(2,1)S(1)}, bf16[4,1,768]{2,1,0:T(2,128)(2,1)S(1)}, u32[]{:S(2)}, u32[]{:S(2)}) collective-permute-start(bf16[4,1,768]{2,1,0:T(2,128)(2,1)S(1)} %slice.243), channel_id=1, source_target_pairs={{0,2},{1,3},{4,6},{5,7},{8,10},{9,11},{12,14},{13,15},{16,18},{17,... | collective-permute-start | bytes 18440 | tf_op jit(solution)/shard_map/ppermute | solution.py:672
  320.5 13.2 %collective-permute-start.26 = (bf16[80,768]{1,0:T(8,128)(2,1)S(1)}, bf16[80,768]{1,0:T(8,128)(2,1)S(1)}, u32[]{:S(2)}, u32[]{:S(2)}) collective-permute-start(bf16[80,768]{1,0:T(8,128)(2,1)S(1)} %get-tuple-element.89), channel_id=1, source_target_pairs={{0,1},{1,0},{2,3},{3,2},{4,5},{5,4},{6,7},{7,6},{8,9},{9,8},{10,11... | collective-permute-start | bytes 368648 | tf_op jit(solution)/shard_map/ppermute | solution.py:629
  320.5 15.2 %collective-permute-start.27 = (bf16[80,768]{1,0:T(8,128)(2,1)S(1)}, bf16[80,768]{1,0:T(8,128)(2,1)S(1)}, u32[]{:S(2)}, u32[]{:S(2)}) collective-permute-start(bf16[80,768]{1,0:T(8,128)(2,1)S(1)} %get-tuple-element.91), channel_id=1, source_target_pairs={{0,2},{1,3},{2,0},{3,1},{4,6},{5,7},{6,4},{7,5},{8,10},{9,11},{10,... | collective-permute-start | bytes 368648 | tf_op jit(solution)/shard_map/ppermute | solution.py:629
  330.4 10.3 %collective-permute-start.28 = (bf16[80,768]{1,0:T(8,128)(2,1)S(1)}, bf16[80,768]{1,0:T(8,128)(2,1)S(1)}, u32[]{:S(2)}, u32[]{:S(2)}) collective-permute-start(bf16[80,768]{1,0:T(8,128)(2,1)S(1)} %get-tuple-element.90), channel_id=1, source_target_pairs={{0,3},{1,2},{2,1},{3,0},{4,7},{5,6},{6,5},{7,4},{8,11},{9,10},{10,... | collective-permute-start | bytes 368648 | tf_op jit(solution)/shard_map/ppermute | solution.py:629
  343.2 11.5 %collective-permute-start.29 = (bf16[216,768]{1,0:T(8,128)(2,1)S(1)}, bf16[216,768]{1,0:T(8,128)(2,1)S(1)}, u32[]{:S(2)}, u32[]{:S(2)}) collective-permute-start(bf16[216,768]{1,0:T(8,128)(2,1)S(1)} %get-tuple-element.84), channel_id=1, source_target_pairs={{0,1},{1,0},{2,3},{3,2},{4,5},{5,4},{6,7},{7,6},{8,9},{9,8},{10,11... | collective-permute-start | bytes 995336 | tf_op jit(solution)/shard_map/ppermute | solution.py:629
  343.3 23.5 %collective-permute-start.30 = (bf16[216,768]{1,0:T(8,128)(2,1)S(1)}, bf16[216,768]{1,0:T(8,128)(2,1)S(1)}, u32[]{:S(2)}, u32[]{:S(2)}) collective-permute-start(bf16[216,768]{1,0:T(8,128)(2,1)S(1)} %get-tuple-element.85), channel_id=1, source_target_pairs={{0,2},{1,3},{2,0},{3,1},{4,6},{5,7},{6,4},{7,5},{8,10},{9,11},{10,... | collective-permute-start | bytes 995336 | tf_op jit(solution)/shard_map/ppermute | solution.py:629
  344.3 30.3 %collective-permute-start.31 = (bf16[216,768]{1,0:T(8,128)(2,1)S(1)}, bf16[216,768]{1,0:T(8,128)(2,1)}, u32[]{:S(2)}, u32[]{:S(2)}) collective-permute-start(bf16[216,768]{1,0:T(8,128)(2,1)S(1)} %get-tuple-element.86), channel_id=1, source_target_pairs={{0,3},{1,2},{2,1},{3,0},{4,7},{5,6},{6,5},{7,4},{8,11},{9,10},{10,... | collective-permute-start | bytes 995336 | tf_op jit(solution)/shard_map/ppermute | solution.py:629
Sparse Core Ops, SparseCore 0:
  62.0 80.2 all-gather.2
  230.8 61.9 reduce-scatter.1
